TPU v7x, 32 devices: a whole 2x2x4 slice. The times are simulated.
32 devices in a mesh: fsdp: 8 (over z, x), seq: 4 (over y, core).
Axes of the slice: x: 2, y: 2, z: 4, core: 2. Of those that a mesh axis runs over, the one named last changes fastest.
Arguments:
- tokens: bfloat16 [24, 580, 768], P('fsdp', 'seq'), may hold values from -6 to 6
- routes: int32 [24, 580, 2], P('fsdp'), may hold values from 0 to 3, all different within a row
- ln1_gain: bfloat16 [768], P(('fsdp', 'seq')), may hold values from 0.5 to 1.5
- ln1_bias: bfloat16 [768], P(('fsdp', 'seq')), may hold values from -3 to 3
- w_qkv: bfloat16 [768, 2304], P(('fsdp', 'seq')), may hold values from -0.3125 to 0.3125
- b_qv: bfloat16 [1536], P(('fsdp', 'seq')), may hold values from -4 to 4
- w_proj: bfloat16 [768, 768], P(('fsdp', 'seq')), may hold values from -0.875 to 0.875
- b_proj: bfloat16 [768], P(('fsdp', 'seq')), may hold values from -4 to 4
- ln2_gain: bfloat16 [768], P(('fsdp', 'seq')), may hold values from 0.5 to 1.5
- ln2_bias: bfloat16 [768], P(('fsdp', 'seq')), may hold values from -3 to 3
- w_router: bfloat16 [768, 4], P(('fsdp', 'seq')), may hold values from -0.15625 to 0.15625
- w_in: bfloat16 [4, 768, 3072], P(None, 'fsdp', 'seq'), may hold values from -0.21875 to 0.21875
- b_in: bfloat16 [12288], P(('fsdp', 'seq')), may hold values from -4 to 4
- w_out: bfloat16 [4, 3072, 768], P(None, 'seq', 'fsdp'), may hold values from -0.3125 to 0.3125
- b_out: bfloat16 [3072], P(('fsdp', 'seq')), may hold values from -1.5 to 1.5
- cotangent: bfloat16 [24, 580, 768], P('fsdp', 'seq'), may hold values from -6 to 6
Outputs:
- mixed: bfloat16 [24, 580, 768], P('fsdp', 'seq')
- grad_tokens: float32 [24, 580, 768], P('fsdp', 'seq')
- grad_ln1_gain: float32 [768], P(('fsdp', 'seq'))
- grad_ln1_bias: float32 [768], P(('fsdp', 'seq'))
- grad_w_qkv: float32 [768, 2304], P(('fsdp', 'seq'))
- grad_b_qv: float32 [1536], P(('fsdp', 'seq'))
- grad_w_proj: float32 [768, 768], P(('fsdp', 'seq'))
- grad_b_proj: float32 [768], P(('fsdp', 'seq'))
- grad_ln2_gain: float32 [768], P(('fsdp', 'seq'))
- grad_ln2_bias: float32 [768], P(('fsdp', 'seq'))
- grad_w_router: float32 [768, 4], P(('fsdp', 'seq'))
- grad_w_in: float32 [4, 768, 3072], P(None, 'fsdp', 'seq')
- grad_b_in: float32 [12288], P(('fsdp', 'seq'))
- grad_w_out: float32 [4, 3072, 768], P(None, 'seq', 'fsdp')
- grad_b_out: float32 [3072], P(('fsdp', 'seq'))
Inputs may be any that keep to these rules, and one draw needn't show every extreme that they name: `routes`: the two experts of a token slot differ, and each of the 4 experts is named by some slot.
All inputs are finite; a program needn't handle non-finite values.
Results may differ from a plain program's by a relative error of at most 0.014.
Values may be sent and summed in bfloat16 or wider, within the bound.
A program may use at most 256 MiB of HBM per device.

v0:
```python
from functools import partial

import jax
import jax.numpy as jnp
from jax import lax
from jax.sharding import PartitionSpec as P

HEAD = 64
TILE = 512


EPSILON = 1e-06
HIGHEST = lax.Precision.HIGHEST


def norm_rows(values, gain_vector, shift_vector):
    average = jnp.mean(values, axis=-1, keepdims=True)
    centred = values - average
    variance = jnp.mean(centred * centred, axis=-1, keepdims=True)
    return centred * lax.rsqrt(variance + EPSILON) * gain_vector + shift_vector


def softmax_last(values):
    return jax.nn.softmax(values, axis=-1)


def gelu_tanh(values):
    return jax.nn.gelu(values, approximate=True)


def masked_scores(queries, keys_now, key_valid):
    head_scale = queries.shape[-1] ** (-0.5)
    scores = (
        jnp.einsum("bqhd,bkhd->bhqk", queries, keys_now, preferred_element_type=jnp.float32)
        * head_scale
    )
    return jnp.where(key_valid, scores, -jnp.inf)


def attend_block(key_valid, qkv_block):
    queries = qkv_block[:, :, 0]
    keys_now = qkv_block[:, :, 1]
    values_now = qkv_block[:, :, 2]
    scores = masked_scores(queries, keys_now, key_valid)
    highest = jnp.max(scores, axis=-1, keepdims=True)
    weights = jnp.exp(scores - highest)
    totals = jnp.sum(weights, axis=-1, keepdims=True)
    probs_low = (weights / totals).astype(jnp.bfloat16)
    attended = jnp.einsum(
        "bhqk,bkhd->bqhd", probs_low, values_now, preferred_element_type=jnp.float32
    )
    return (attended.astype(jnp.bfloat16), (highest + jnp.log(totals))[..., 0])


def attend_back(key_valid, pieces):
    qkv_block, grad_block, log_block = pieces
    queries = qkv_block[:, :, 0]
    keys_now = qkv_block[:, :, 1]
    values_now = qkv_block[:, :, 2]
    head_scale = queries.shape[-1] ** (-0.5)
    scores = masked_scores(queries, keys_now, key_valid)
    probs = jnp.exp(scores - log_block[..., None])
    grad_probs = jnp.einsum(
        "bqhd,bkhd->bhqk", grad_block, values_now, preferred_element_type=jnp.float32
    )
    grad_values = jnp.einsum(
        "bhqk,bqhd->bkhd",
        probs.astype(jnp.bfloat16),
        grad_block,
        preferred_element_type=jnp.float32,
    )
    inner = jnp.sum(probs * grad_probs, axis=-1, keepdims=True)
    grad_scores = (probs * (grad_probs - inner)).astype(jnp.bfloat16)
    grad_queries = (
        jnp.einsum("bhqk,bkhd->bqhd", grad_scores, keys_now, preferred_element_type=jnp.float32)
        * head_scale
    )
    grad_keys = (
        jnp.einsum("bhqk,bqhd->bkhd", grad_scores, queries, preferred_element_type=jnp.float32)
        * head_scale
    )
    return jnp.stack([grad_queries, grad_keys, grad_values], axis=2).astype(jnp.bfloat16)


def expert_pass(rows_now, grad_now, inner_now, outer_now, bias_now):
    pre_now = jnp.dot(rows_now, inner_now, preferred_element_type=jnp.float32) + bias_now
    active_now = gelu_tanh(pre_now).astype(jnp.bfloat16)
    result = jnp.einsum("tq,dq->td", active_now, outer_now, preferred_element_type=jnp.float32)
    grad_active = jnp.dot(grad_now, outer_now, preferred_element_type=jnp.float32)
    _, gelu_pull = jax.vjp(gelu_tanh, pre_now)
    grad_pre = gelu_pull(grad_active)[0].astype(jnp.bfloat16)
    inner_grad = jnp.einsum("td,tq->dq", rows_now, grad_pre, preferred_element_type=jnp.float32)
    outer_grad = jnp.einsum("td,tq->dq", grad_now, active_now, preferred_element_type=jnp.float32)
    bias_grad = jnp.sum(grad_pre.astype(jnp.float32), axis=0)
    grad_rows_now = jnp.einsum("tq,dq->td", grad_pre, inner_now, preferred_element_type=jnp.float32)
    return (result, grad_rows_now, inner_grad, outer_grad, bias_grad)


def per_device(
    tokens,
    routes,
    ln1_gain,
    ln1_bias,
    w_qkv,
    b_qv,
    w_proj,
    b_proj,
    ln2_gain,
    ln2_bias,
    w_router,
    w_in,
    b_in,
    w_out,
    b_out,
    cotangent,
):
    seq_count = lax.axis_size("seq")
    seq_place = lax.axis_index("seq")
    images, slots, width = tokens.shape
    experts = w_in.shape[0]
    quarter = w_in.shape[2]
    length = seq_count * slots
    head_local = width // HEAD // seq_count
    local_width = head_local * HEAD
    (
        gain_one,
        shift_one,
        qkv_weight,
        qv_shift,
        proj_weight,
        proj_shift,
        gain_two,
        shift_two,
        router_weight,
        inner_shift,
        outer_shift,
    ) = (
        lax.all_gather(ln1_gain, ("fsdp", "seq"), axis=0, tiled=True),
        lax.all_gather(ln1_bias, ("fsdp", "seq"), axis=0, tiled=True),
        lax.all_gather(w_qkv, ("fsdp", "seq"), axis=0, tiled=True),
        lax.all_gather(b_qv, ("fsdp", "seq"), axis=0, tiled=True),
        lax.all_gather(w_proj, ("fsdp", "seq"), axis=0, tiled=True),
        lax.all_gather(b_proj, ("fsdp", "seq"), axis=0, tiled=True),
        lax.all_gather(ln2_gain, ("fsdp", "seq"), axis=0, tiled=True),
        lax.all_gather(ln2_bias, ("fsdp", "seq"), axis=0, tiled=True),
        lax.all_gather(w_router, ("fsdp", "seq"), axis=0, tiled=True),
        lax.all_gather(b_in, ("fsdp", "seq"), axis=0, tiled=True),
        lax.all_gather(b_out, ("fsdp", "seq"), axis=0, tiled=True),
    )
    gain_one = gain_one.astype(jnp.float32)
    shift_one = shift_one.astype(jnp.float32)
    gain_two = gain_two.astype(jnp.float32)
    shift_two = shift_two.astype(jnp.float32)
    slot_index = jnp.arange(slots)
    own_valid = ((seq_place == 0) | (slot_index < slots - 1))[None, :, None]
    places = jnp.arange(length)
    key_valid = (places < slots) | (places % slots < slots - 1)
    inner_all = inner_shift.reshape(experts, -1).astype(jnp.float32)
    outer_bias = outer_shift.reshape(experts, width).astype(jnp.float32)
    outer_local = jnp.swapaxes(w_out, 1, 2)
    inner_bias = lax.dynamic_slice_in_dim(inner_all, seq_place * quarter, quarter, 1)
    inner_weight, outer_weight = (
        lax.all_gather(w_in, "fsdp", axis=1, tiled=True),
        lax.all_gather(outer_local, "fsdp", axis=1, tiled=True),
    )
    inputs32 = tokens.astype(jnp.float32)
    normed_one = norm_rows(inputs32, gain_one, shift_one).astype(jnp.bfloat16)
    qv32 = qv_shift.astype(jnp.float32)
    qkv_bias = jnp.concatenate([qv32[:width], jnp.zeros((width,), jnp.float32), qv32[width:]])
    qkv = (
        jnp.einsum("btd,de->bte", normed_one, qkv_weight, preferred_element_type=jnp.float32)
        + qkv_bias
    )
    qkv_split = qkv.astype(jnp.bfloat16).reshape(images, slots, 3, seq_count, local_width)
    qkv_heads = lax.all_to_all(qkv_split, "seq", split_axis=3, concat_axis=1, tiled=True)
    blocks = qkv_heads.reshape(1, images, length, 3, head_local, HEAD)
    attended_heads, log_totals = lax.map(partial(attend_block, key_valid), blocks)
    attended_back = lax.all_to_all(
        attended_heads.reshape(images, length, 1, local_width),
        "seq",
        split_axis=1,
        concat_axis=2,
        tiled=True,
    )
    attended_tok = attended_back.reshape(images, slots, width)
    branch = jnp.einsum(
        "btd,de->bte", attended_tok, proj_weight, preferred_element_type=jnp.float32
    )
    middle = inputs32 + branch + proj_shift.astype(jnp.float32)
    normed_two = norm_rows(middle, gain_two, shift_two).astype(jnp.bfloat16)
    logits = jnp.einsum(
        "btd,de->bte", normed_two, router_weight, preferred_element_type=jnp.float32
    )
    router = softmax_last(logits)
    routes_own = lax.dynamic_slice_in_dim(routes, seq_place * slots, slots, 1)
    expert_ids = jnp.arange(experts)
    chosen_own = (routes_own[..., None] == expert_ids).astype(jnp.float32)
    gates = jnp.sum(chosen_own * router[:, :, None, :], axis=-1).astype(jnp.bfloat16)
    gates32 = gates.astype(jnp.float32)
    grad_out = jnp.where(own_valid, cotangent, jnp.zeros((), jnp.bfloat16))
    grad32 = grad_out.astype(jnp.float32)
    group_rows, group_gates, group_grad = (
        lax.all_gather(normed_two, "seq", axis=1, tiled=True),
        lax.all_gather(gates, "seq", axis=1, tiled=True),
        lax.all_gather(grad_out, "seq", axis=1, tiled=True),
    )
    token_count = images * length
    entry_expert = routes.reshape(-1)
    entry_total = entry_expert.shape[0]
    tile_count = (entry_total + experts * (TILE - 1)) // TILE
    order = jnp.argsort(entry_expert, stable=True)
    inverse = jnp.argsort(order)
    entry_onehot = entry_expert[:, None] == expert_ids
    counts = jnp.sum(entry_onehot.astype(jnp.int32), axis=0)
    padded = (counts + TILE - 1) // TILE * TILE
    padded_end = jnp.cumsum(padded)
    padded_start = padded_end - padded
    count_end = jnp.cumsum(counts)
    count_start = count_end - counts
    slot_place = jnp.arange(tile_count * TILE)
    slot_expert = jnp.sum((padded_end[None, :] <= slot_place[:, None]).astype(jnp.int32), axis=1)
    slot_onehot = slot_expert[:, None] == expert_ids
    slot_rank = slot_place - jnp.sum(jnp.where(slot_onehot, padded_start, 0), axis=1)
    slot_live = (slot_expert < experts) & (
        slot_rank < jnp.sum(jnp.where(slot_onehot, counts, 0), axis=1)
    )
    sorted_index = jnp.clip(
        jnp.sum(jnp.where(slot_onehot, count_start, 0), axis=1) + slot_rank, 0, entry_total - 1
    )
    slot_entry = order[sorted_index]
    slot_token = slot_entry // 2
    tile_expert = jnp.minimum(slot_expert.reshape(tile_count, TILE)[:, 0], experts - 1)
    entry_slot = jnp.sum(jnp.where(entry_onehot, padded_start - count_start, 0), axis=1) + inverse
    rows_flat = group_rows.reshape(token_count, width)
    grad_flat = group_grad.reshape(token_count, width)
    slot_rows = jnp.where(slot_live[:, None], rows_flat[slot_token], jnp.zeros((), jnp.bfloat16))
    slot_gate = jnp.where(slot_live, group_gates.reshape(-1)[slot_entry].astype(jnp.float32), 0.0)
    slot_grad = (slot_gate[:, None] * grad_flat[slot_token].astype(jnp.float32)).astype(
        jnp.bfloat16
    )

    def expert_tile(totals, pieces):
        inner_sum, outer_sum, bias_sum = totals
        rows_now, grad_now, expert_now = pieces
        result, grad_rows_now, inner_part, outer_part, bias_part = expert_pass(
            rows_now,
            grad_now,
            inner_weight[expert_now],
            outer_weight[expert_now],
            inner_bias[expert_now],
        )
        inner_sum = inner_sum.at[expert_now].add(inner_part)
        outer_sum = outer_sum.at[expert_now].add(outer_part)
        bias_sum = bias_sum.at[expert_now].add(bias_part)
        return ((inner_sum, outer_sum, bias_sum), (result, grad_rows_now))

    initial = (
        jnp.zeros((experts, width, quarter), jnp.float32),
        jnp.zeros((experts, width, quarter), jnp.float32),
        jnp.zeros((experts, quarter), jnp.float32),
    )
    (inner_grad, outer_grad, inner_bias_grad), (slot_out, slot_back) = lax.scan(
        expert_tile,
        initial,
        (
            slot_rows.reshape(tile_count, TILE, width),
            slot_grad.reshape(tile_count, TILE, width),
            tile_expert,
        ),
    )
    entry_out = slot_out.reshape(-1, width)[entry_slot].reshape(token_count, 2, width)
    entry_gate = group_gates.reshape(token_count, 2).astype(jnp.float32)
    partial_mix = jnp.sum(entry_gate[..., None] * entry_out, axis=1).reshape(images, length, width)
    partial_rows = jnp.sum(
        slot_back.reshape(-1, width)[entry_slot].reshape(token_count, 2, width), axis=1
    )
    entry_dot = jnp.sum(grad_flat.astype(jnp.float32)[:, None, :] * entry_out, axis=-1)
    expert_mix, row_grad, gate_grad = (
        lax.psum_scatter(
            partial_mix.astype(jnp.bfloat16), "seq", scatter_dimension=1, tiled=True
        ).astype(jnp.float32),
        lax.psum_scatter(
            partial_rows.reshape(images, length, width).astype(jnp.bfloat16),
            "seq",
            scatter_dimension=1,
            tiled=True,
        ).astype(jnp.float32),
        lax.psum_scatter(
            entry_dot.reshape(images, length, 2).astype(jnp.bfloat16),
            "seq",
            scatter_dimension=1,
            tiled=True,
        ).astype(jnp.float32),
    )
    inner_bias_full = lax.dynamic_update_slice_in_dim(
        jnp.zeros((experts, quarter * seq_count), jnp.float32),
        inner_bias_grad,
        seq_place * quarter,
        1,
    ).reshape(-1)
    gated_choice = chosen_own * gates32[..., None]
    bias_mix = jnp.einsum("bske,ed->bsd", gated_choice, outer_bias, precision=HIGHEST)
    output32 = middle + expert_mix + bias_mix
    mixed = jnp.where(own_valid, output32, 0.0).astype(jnp.bfloat16)
    gate_grad = gate_grad + jnp.einsum(
        "bsd,bske,ed->bsk", grad32, chosen_own, outer_bias, precision=HIGHEST
    )
    grad_router_probs = jnp.einsum("bsk,bske->bse", gate_grad, chosen_own, precision=HIGHEST)
    _, soft_pull = jax.vjp(softmax_last, logits)
    grad_logits = soft_pull(grad_router_probs)[0]
    router_grad = jnp.einsum(
        "bsd,bse->de", normed_two.astype(jnp.float32), grad_logits, precision=HIGHEST
    )
    grad_normed_two = row_grad + jnp.einsum(
        "bse,de->bsd", grad_logits, router_weight.astype(jnp.float32), precision=HIGHEST
    )
    outer_bias_grad = jnp.einsum("bske,bsd->ed", gated_choice, grad32, precision=HIGHEST)
    _, norm_pull_two = jax.vjp(norm_rows, middle, gain_two, shift_two)
    grad_middle_norm, grad_gain_two, grad_shift_two = norm_pull_two(grad_normed_two)
    grad_middle = grad32 + grad_middle_norm
    grad_branch = grad_middle.astype(jnp.bfloat16)
    proj_shift_grad = jnp.sum(grad_branch.astype(jnp.float32), axis=(0, 1))
    proj_weight_grad = jnp.einsum(
        "bsd,bse->de", attended_tok, grad_branch, preferred_element_type=jnp.float32
    )
    grad_attended = jnp.einsum(
        "bse,de->bsd", grad_branch, proj_weight, preferred_element_type=jnp.float32
    ).astype(jnp.bfloat16)
    grad_heads = lax.all_to_all(
        grad_attended.reshape(images, slots, seq_count, local_width),
        "seq",
        split_axis=2,
        concat_axis=1,
        tiled=True,
    )
    grad_blocks = grad_heads.reshape(1, images, length, head_local, HEAD)
    grad_qkv_heads = lax.map(partial(attend_back, key_valid), (blocks, grad_blocks, log_totals))
    grad_qkv_back = lax.all_to_all(
        grad_qkv_heads.reshape(images, length, 3, 1, local_width),
        "seq",
        split_axis=1,
        concat_axis=3,
        tiled=True,
    )
    grad_qkv = grad_qkv_back.reshape(images, slots, 3 * width)
    qkv_weight_grad = jnp.einsum(
        "bsd,bse->de", normed_one, grad_qkv, preferred_element_type=jnp.float32
    )
    qkv_columns = jnp.sum(grad_qkv.astype(jnp.float32), axis=(0, 1))
    qv_grad = jnp.concatenate([qkv_columns[:width], qkv_columns[2 * width :]])
    grad_normed_one = jnp.einsum(
        "bse,de->bsd", grad_qkv, qkv_weight, preferred_element_type=jnp.float32
    )
    _, norm_pull_one = jax.vjp(norm_rows, inputs32, gain_one, shift_one)
    grad_input_norm, grad_gain_one, grad_shift_one = norm_pull_one(grad_normed_one)
    grad_tokens = jnp.where(own_valid, grad_middle + grad_input_norm, 0.0)
    (
        grad_ln1_gain,
        grad_ln1_bias,
        grad_w_qkv,
        grad_b_qv,
        grad_w_proj,
        grad_b_proj,
        grad_ln2_gain,
        grad_ln2_bias,
        grad_w_router,
        grad_b_in,
        grad_b_out,
    ) = (
        lax.psum_scatter(grad_gain_one, ("fsdp", "seq"), scatter_dimension=0, tiled=True),
        lax.psum_scatter(grad_shift_one, ("fsdp", "seq"), scatter_dimension=0, tiled=True),
        lax.psum_scatter(qkv_weight_grad, ("fsdp", "seq"), scatter_dimension=0, tiled=True),
        lax.psum_scatter(qv_grad, ("fsdp", "seq"), scatter_dimension=0, tiled=True),
        lax.psum_scatter(proj_weight_grad, ("fsdp", "seq"), scatter_dimension=0, tiled=True),
        lax.psum_scatter(proj_shift_grad, ("fsdp", "seq"), scatter_dimension=0, tiled=True),
        lax.psum_scatter(grad_gain_two, ("fsdp", "seq"), scatter_dimension=0, tiled=True),
        lax.psum_scatter(grad_shift_two, ("fsdp", "seq"), scatter_dimension=0, tiled=True),
        lax.psum_scatter(router_grad, ("fsdp", "seq"), scatter_dimension=0, tiled=True),
        lax.psum_scatter(inner_bias_full, ("fsdp", "seq"), scatter_dimension=0, tiled=True),
        lax.psum_scatter(
            outer_bias_grad.reshape(-1), ("fsdp", "seq"), scatter_dimension=0, tiled=True
        ),
    )
    grad_w_in, outer_owned = (
        lax.psum_scatter(inner_grad, "fsdp", scatter_dimension=1, tiled=True),
        lax.psum_scatter(outer_grad, "fsdp", scatter_dimension=1, tiled=True),
    )
    grad_w_out = jnp.swapaxes(outer_owned, 1, 2)
    return (
        mixed,
        grad_tokens,
        grad_ln1_gain,
        grad_ln1_bias,
        grad_w_qkv,
        grad_b_qv,
        grad_w_proj,
        grad_b_proj,
        grad_ln2_gain,
        grad_ln2_bias,
        grad_w_router,
        grad_w_in,
        grad_b_in,
        grad_w_out,
        grad_b_out,
    )


def solution(mesh):
    in_specs = (
        P("fsdp", "seq", None),
        P("fsdp", None, None),
        P(("fsdp", "seq")),
        P(("fsdp", "seq")),
        P(("fsdp", "seq"), None),
        P(("fsdp", "seq")),
        P(("fsdp", "seq"), None),
        P(("fsdp", "seq")),
        P(("fsdp", "seq")),
        P(("fsdp", "seq")),
        P(("fsdp", "seq"), None),
        P(None, "fsdp", "seq"),
        P(("fsdp", "seq")),
        P(None, "seq", "fsdp"),
        P(("fsdp", "seq")),
        P("fsdp", "seq", None),
    )
    out_specs = (
        P("fsdp", "seq", None),
        P("fsdp", "seq", None),
        P(("fsdp", "seq")),
        P(("fsdp", "seq")),
        P(("fsdp", "seq"), None),
        P(("fsdp", "seq")),
        P(("fsdp", "seq"), None),
        P(("fsdp", "seq")),
        P(("fsdp", "seq")),
        P(("fsdp", "seq")),
        P(("fsdp", "seq"), None),
        P(None, "fsdp", "seq"),
        P(("fsdp", "seq")),
        P(None, "seq", "fsdp"),
        P(("fsdp", "seq")),
    )
    return jax.shard_map(
        per_device, mesh=mesh, in_specs=in_specs, out_specs=out_specs, check_vma=False
    )
```

profile of v0, /device:TPU:25, one launch (start us, length us, event | category | flops | bytes accessed | tf_op | source)
XLA Modules:
  0.0 1744.5 jit_solution(12413642278299522418)
XLA Ops:
  14.6 39.2 %all-reduce.20 = (bf16[3072]{0:T(1024)(128)(2,1)}, bf16[1536]{0:T(1024)(128)(2,1)S(1)}, bf16[768]{0:T(1024)(128)(2,1)S(1)}, bf16[768]{0:T(1024)(128)(2,1)S(1)}, ...) all-reduce(bf16[3072]{0:T(1024)(128)(2,1)S(1)} %dynamic-update-slic, ...), channel_id=1, replica_groups=mesh['fsdp'=8,'seq'=4] {'fsdp','seq'}, use_global_device_ids=true, to_apply=%add.6 | all-reduce | flops 8448 | bytes 33792
  57.3 14.1 all-gather.9.cloned.1.call-done
  71.4 5.5 fusion.42
  90.2 31.7 %all-to-all-done = bf16[3,145,3,4,192]{4,1,2,0,3:T(8,128)(2,1)S(1)} async-done(((bf16[3,145,3,4,192]{4,1,2,0,3:T(8,128)(2,1)}), bf16[3,145,3,4,192]{4,1,2,0,3:T(8,128)(2,1)S(1)}, u32[]{:S(2)}, u32[]{:S(2)}) %all-to-all-start) | async-done | bytes 2004512 | tf_op jit(solution)/shard_map/all_to_all | solution.py:175
  121.9 5.1 copy.206
  127.1 5.9 reshape.744
  152.8 20.0 %all-to-all-done.1 = bf16[3,580,1,192]{3,0,2,1:T(4,128)(2,1)S(1)} async-done(((bf16[3,580,1,192]{3,0,2,1:T(4,128)(2,1)}), bf16[3,580,1,192]{3,0,2,1:T(4,128)(2,1)S(1)}, u32[]{:S(2)}, u32[]{:S(2)}) %all-to-all-start.1) | async-done | bytes 668192 | tf_op jit(solution)/shard_map/all_to_all | solution.py:178
  180.6 32.8 %all-gather = bf16[32,24,4]{1,2,0:T(4,128)(2,1)S(1)} all-gather(bf16[1,24,4]{1,2,0:T(4,128)(2,1)S(1)} %bitcast.234), channel_id=1, replica_groups=mesh['fsdp'=8,'seq'=4] {'fsdp','seq'}, dimensions={0}, use_global_device_ids=true | all-gather | bytes 6336 | tf_op jit(solution)/shard_map/all_gather | solution.py:146
  215.4 5.9 sort.34
  221.7 37.9 %all-gather.1 = bf16[32,1,384]{2,1,0:T(2,128)(2,1)S(1)} all-gather(bf16[1,1,384]{2,1,0:T(2,128)(2,1)S(1)} %reshape.715), channel_id=1, replica_groups=mesh['fsdp'=8,'seq'=4] {'fsdp','seq'}, dimensions={0}, use_global_device_ids=true | all-gather | bytes 25344 | tf_op jit(solution)/shard_map/all_gather | solution.py:147
  259.8 28.7 %gather_fusion = s32[5120]{0:T(1024)S(1)} fusion(s32[3480]{0:T(1024)S(1)} %get-tuple-element.239, s32[5120]{0:T(1024)S(1)} %broadcast_clamp_fusion.2), kind=kCustom, calls=%fused_computation | custom fusion | bytes 61440 | tf_op jit(solution)/shard_map/gather | solution.py:230
  288.5 5.9 sort.35
  304.0 21.9 %gather_fusion.3 = bf16[5120,768]{1,0:T(8,128)(2,1)} fusion(bf16[1740,768]{1,0:T(8,128)(2,1)S(1)} %reshape.635, s32[5120]{0:T(1024)S(1)} %broadcast_clamp_fusion), kind=kCustom, calls=%fused_computation.3 | custom fusion | bytes 15749120 | tf_op jit(solution)/shard_map/gather | solution.py:238
  328.3 7.5 all_gather.57
  340.9 31.9 %gather_fusion.2 = bf16[5120]{0:T(1024)(128)(2,1)S(1)} fusion(bf16[3480]{0:T(1024)(128)(2,1)S(1)} %reshape.634, s32[5120]{0:T(1024)S(1)} %broadcast_clamp_fusion.1), kind=kCustom, calls=%fused_computation.2 | custom fusion | bytes 40960 | tf_op jit(solution)/shard_map/gather | solution.py:237
  374.2 7.7 fusion.35
  387.8 22.1 %gather_fusion.1 = bf16[5120,768]{1,0:T(8,128)(2,1)} fusion(bf16[1740,768]{1,0:T(8,128)(2,1)S(1)} %reshape.632, s32[5120]{0:T(1024)S(1)} %broadcast_clamp_fusion), kind=kCustom, calls=%fused_computation.1 | custom fusion | bytes 15749120 | tf_op jit(solution)/shard_map/gather | solution.py:236
  410.0 7.0 broadcast_select_fusion.1
  425.8 256.3 %while.7 = (s32[]{:T(128)}, f32[4,768,768]{2,1,0:T(8,128)}, f32[4,768,768]{2,1,0:T(8,128)}, f32[4,768]{1,0:T(4,128)S(1)}, f32[10,512,768]{2,1,0:T(8,128)}, /*ind...) while((s32[]{:T(128)}, f32[4,768,768]{2,1,0:T(8,128)}, ...), condition=%wide.region_21.22_spmd, body=%wide.region_17.21_spmd.sunk | while | flops 3642360576 | bytes 48007456 | solution.py:262
  440.3 4.8 fusion.136
  445.1 4.9 fusion.137
  465.9 4.8 fusion.136
  470.7 4.9 fusion.137
  491.5 4.8 fusion.136
  496.3 4.9 fusion.137
  517.1 4.8 fusion.136
  521.9 4.9 fusion.137
  542.7 4.8 fusion.136
  547.6 4.9 fusion.137
  568.3 4.8 fusion.136
  573.2 4.9 fusion.137
  593.9 4.9 fusion.136
  598.8 4.9 fusion.137
  619.6 4.9 fusion.136
  624.4 4.9 fusion.137
  645.2 4.9 fusion.136
  650.1 4.9 fusion.137
  670.9 4.9 fusion.136
  675.8 4.9 fusion.137
  682.2 19.5 %gather_fusion.4 = f32[3480,768]{1,0:T(8,128)} fusion(f32[5120,768]{1,0:T(8,128)} %bitcast.36, s32[4096]{0:T(1024)S(1)} %pad_clamp_fusion), kind=kCustom, calls=%fused_computation.4 | custom fusion | bytes 21395040 | tf_op jit(solution)/shard_map/gather | solution.py:271
  701.7 12.9 reshape.637
  714.6 23.5 %multiply_reduce_fusion.1 = (bf16[1740,2]{1,0:T(8,128)(2,1)S(1)}, bf16[1740,768]{1,0:T(8,128)(2,1)S(1)}) fusion(f32[1740,2,768]{2,1,0:T(2,128)} %reshape.637, f32[1740,768]{1,0:T(8,128)} %convert_element_type.224, f32[1740,2]{1,0:T(8,128)} %copy.161), kind=kLoop, calls=%fused_computation.61 | loop fusion | flops 9350760 | bytes 18729360 | tf_op jit(solution)/shard_map/reduce_sum | solution.py:277
  740.0 19.3 %gather_fusion.5 = f32[3480,768]{1,0:T(8,128)} fusion(f32[5120,768]{1,0:T(8,128)} %bitcast.211, s32[4096]{0:T(1024)S(1)} %pad_clamp_fusion), kind=kCustom, calls=%fused_computation.5 | custom fusion | bytes 21395040 | tf_op jit(solution)/shard_map/gather | solution.py:275
  759.4 12.9 reshape.640
  772.3 14.2 reduce_sum.368
  791.1 9.4 all-reduce.9
  800.6 97.3 %all-reduce.27.cloned.1.call-done = (bf16[3,580,768]{2,1,0:T(8,128)(2,1)}, bf16[3,580,768]{2,1,0:T(8,128)(2,1)}) async-done(((bf16[3,580,768]{2,1,0:T(8,128)(2,1)}, bf16[3,580,768]{2,1,0:T(8,128)(2,1)}), (bf16[3,580,768]{2,1,0:T(8,128)(2,1)}, bf16[3,580,768]{2,1,0:T(8,128)(2,1)})) %all-reduce.27.cloned.1.call-update) | async-done | bytes 5345296
  909.4 5.3 all-to-all-start.2
  914.7 12.4 all-to-all-done.2
  933.7 12.8 multiply_reduce_fusion
  946.5 6.7 multiply_convert_fusion.3
  961.3 5.0 copy.174
  969.8 5.0 copy.176
  974.8 9.3 pad_maximum_fusion
  984.1 5.7 all-to-all-start.3
  992.5 37.9 %all-to-all-done.3 = bf16[3,580,3,1,192]{4,2,0,3,1:T(4,128)(2,1)} async-done(((bf16[3,580,3,1,192]{4,2,0,3,1:T(4,128)(2,1)}), bf16[3,580,3,1,192]{4,2,0,3,1:T(4,128)(2,1)}, u32[]{:S(2)}, u32[]{:S(2)}) %all-to-all-start.3) | async-done | bytes 2004512 | tf_op jit(solution)/shard_map/all_to_all | solution.py:338
  1036.0 5.6 reshape.642
  1041.7 5.2 fusion.84
  1053.3 6.8 convolution_bitcast_fusion
  1067.9 106.2 %all-reduce.25.cloned.1.call-done = (f32[768]{0:T(1024)}, f32[768]{0:T(1024)}, f32[1536]{0:T(1024)}, f32[768]{0:T(1024)}, f32[768]{0:T(1024)}, /*index=5*/f32[76...) async-done(((f32[768]{0:T(1024)}, f32[768]{0:T(1024)}, f32[1536]{0:T(1024)}, f32[768]{0:T(1024)}, f32[768]{0:T(1024)}, /*index=5*/f32[768]{0:T(1024)}, ...) | async-done | bytes 95248
  1185.5 92.4 %reduce-scatter.11.cloned.1.call-done = f32[24,768]{1,0:T(8,128)} async-done(((f32[768,768]{1,0:T(8,128)}), f32[24,768]{1,0:T(8,128)}) %reduce-scatter.11.cloned.1.call-update) | async-done | bytes 73744 | tf_op jit(solution)/shard_map/reduce_scatter | solution.py:374
  1278.0 125.3 %reduce-scatter.9.cloned.1.call-done = f32[24,2304]{1,0:T(8,128)} async-done(((f32[768,2304]{1,0:T(8,128)}), f32[24,2304]{1,0:T(8,128)}) %reduce-scatter.9.cloned.1.call-update) | async-done | bytes 221200 | tf_op jit(solution)/shard_map/reduce_scatter | solution.py:372
  1403.3 167.6 %reduce-scatter.15.cloned.1.call-done = f32[4,96,768]{2,1,0:T(8,128)} async-done(((f32[4,768,768]{2,1,0:T(8,128)}), f32[4,96,768]{2,1,0:T(8,128)}) %reduce-scatter.15.cloned.1.call-update) | async-done | bytes 1179664 | tf_op jit(solution)/shard_map/reduce_scatter | solution.py:386
  1570.8 166.6 %reduce-scatter.13.cloned.1.call-done = f32[4,96,768]{2,1,0:T(8,128)} async-done(((f32[4,768,768]{2,1,0:T(8,128)}), f32[4,96,768]{2,1,0:T(8,128)}) %reduce-scatter.13.cloned.1.call-update) | async-done | bytes 1179664 | tf_op jit(solution)/shard_map/reduce_scatter | solution.py:385
  (442 shorter events, 294.9 us)
Async XLA Ops:
  7.2 64.2 %all-gather.9.cloned.1.call-start = ((), (), s32[]{:S(2)}) async-start(), calls=%async_computation.8 | async-start | bytes 3649536 | tf_op jit(solution)/shard_map/all_gather | solution.py:140
  7.9 166.4 %all-gather.11.cloned.1.call-start = ((), (), s32[]{:S(2)}) async-start(), calls=%async_computation.9 | async-start | bytes 1216512 | tf_op jit(solution)/shard_map/all_gather | solution.py:142
  55.1 16.3 copy-start.38
  56.7 14.7 copy-start.45
  56.7 14.7 copy-start.57
  57.3 14.1 copy-start.47
  82.9 5.0 copy-start.13
  82.9 39.0 %all-to-all-start = ((bf16[3,145,3,4,192]{4,1,2,0,3:T(8,128)(2,1)}), bf16[3,145,3,4,192]{4,1,2,0,3:T(8,128)(2,1)S(1)}, u32[]{:S(2)}, u32[]{:S(2)}) async-start(bf16[3,145,3,4,192]{4,1,2,0,3:T(8,128)(2,1)} %copy.148), calls=%async_computation | async-start | bytes 5603328 | tf_op jit(solution)/shard_map/all_to_all | solution.py:175
  86.9 208.5 %all-gather.15.cloned.1.call-start = ((), (), s32[]{:S(2)}) async-start(), calls=%async_computation.11 | async-start | bytes 4454400 | tf_op jit(solution)/shard_map/all_gather | solution.py:205
  132.9 4.8 copy-start.3
  135.8 5.7 copy-start
  135.8 5.6 copy-start.24
  141.4 3.5 copy-start.26
  148.2 24.5 %all-to-all-start.1 = ((bf16[3,580,1,192]{3,0,2,1:T(4,128)(2,1)}), bf16[3,580,1,192]{3,0,2,1:T(4,128)(2,1)S(1)}, u32[]{:S(2)}, u32[]{:S(2)}) async-start(bf16[3,580,1,192]{3,0,2,1:T(4,128)(2,1)} %copy.154), calls=%async_computation.1 | async-start | bytes 2375680 | tf_op jit(solution)/shard_map/all_to_all | solution.py:178
  152.5 229.4 %all-gather.13.cloned.1.call-start = ((), (), s32[]{:S(2)}) async-start(), calls=%async_computation.10 | async-start | bytes 4454400 | tf_op jit(solution)/shard_map/all_gather | solution.py:203
  152.7 25.0 %copy-start.34 = (f32[768]{0:T(1024)}, f32[768]{0:T(1024)S(1)}, u32[]{:S(2)}) copy-start(f32[768]{0:T(1024)S(1)} %convert_element_type.200) | copy-start | bytes 9220
  178.0 147.9 %copy-start.10 = (bf16[3,145,768]{2,1,0:T(8,128)(2,1)}, bf16[3,145,768]{2,1,0:T(8,128)(2,1)S(1)}, u32[]{:S(2)}) copy-start(bf16[3,145,768]{2,1,0:T(8,128)(2,1)S(1)} %add_convert_fusion) | copy-start | bytes 2004484
  178.1 36.1 %copy-start.49 = (s32[3,580,2]{1,2,0:T(2,128)S(1)}, s32[3,580,2]{1,2,0:T(2,128)}, u32[]{:S(2)}) copy-start(s32[3,580,2]{1,2,0:T(2,128)} %param.25) | copy-start | bytes 41764
  179.4 42.3 %copy-start.60 = (bf16[384]{0:T(512)(128)(2,1)S(1)}, bf16[384]{0:T(512)(128)(2,1)}, u32[]{:S(2)}) copy-start(bf16[384]{0:T(512)(128)(2,1)} %param.36) | copy-start | bytes 2308
  179.4 237.6 %all-gather.17.cloned.1.call-start = ((), (), s32[]{:S(2)}) async-start(), calls=%async_computation.12 | async-start | bytes 5308416 | tf_op jit(solution)/shard_map/all_gather | solution.py:164
  180.0 237.0 %all-gather.19.cloned.1.call-start = ((), (), s32[]{:S(2)}) async-start(), calls=%async_computation.13 | async-start | bytes 5308416 | tf_op jit(solution)/shard_map/all_gather | solution.py:163
  180.5 717.4 %all-reduce.27.cloned.1.call-start = ((), (), s32[]{:S(2)}) async-start(), calls=%async_computation.19 | async-start | bytes 10764288
  294.5 32.5 %copy-start.32 = (s32[3,145,2]{1,2,0:T(2,128)}, s32[3,145,2]{1,2,0:T(2,128)S(1)}, u32[]{:S(2)}) copy-start(s32[3,145,2]{1,2,0:T(2,128)S(1)} %constant_dynamic-slice_fusion.2) | copy-start | bytes 10444
  421.4 4.4 copy-start.52
  421.4 4.4 copy-start.53
  421.4 4.4 copy-start.61
  428.4 2.9 copy-start.62
  454.0 2.9 copy-start.62
  479.6 2.9 copy-start.62
  505.2 2.9 copy-start.62
  530.8 2.9 copy-start.62
  556.5 2.9 copy-start.62
  582.1 2.9 copy-start.62
  607.7 2.9 copy-start.62
  788.4 12.1 copy-start.23
  788.4 109.5 %copy-start.2 = (f32[3,145,768]{2,1,0:T(8,128)S(1)}, f32[3,145,768]{2,1,0:T(8,128)}, u32[]{:S(2)}) copy-start(f32[3,145,768]{2,1,0:T(8,128)} %copy-done.1) | copy-start | bytes 4008964
  788.5 109.5 %copy-start.29 = (f32[3,145]{1,0:T(4,128)S(1)}, f32[3,145]{1,0:T(4,128)}, u32[]{:S(2)}) copy-start(f32[3,145]{1,0:T(4,128)} %copy-done.28) | copy-start | bytes 5224
  788.5 109.5 %copy-start.35 = (f32[768]{0:T(1024)S(1)}, f32[768]{0:T(1024)}, u32[]{:S(2)}) copy-start(f32[768]{0:T(1024)} %copy-done.34) | copy-start | bytes 9220
  788.5 109.5 %copy-start.37 = (f32[3,145]{1,0:T(4,128)S(1)}, f32[3,145]{1,0:T(4,128)}, u32[]{:S(2)}) copy-start(f32[3,145]{1,0:T(4,128)} %copy-done.36) | copy-start | bytes 5224
  788.5 109.4 %copy-start.40 = (bf16[768,4,1]{0,1,2:T(4,128)(2,1)S(1)}, bf16[768,4,1]{0,1,2:T(4,128)(2,1)}, u32[]{:S(2)}) copy-start(bf16[768,4,1]{0,1,2:T(4,128)(2,1)} %reshape.721) | copy-start | bytes 18436
  897.9 3.2 copy-start.44
  907.1 7.5 copy-start.25
  907.1 7.6 copy-start.27
  909.4 17.7 %all-to-all-start.2 = ((bf16[3,145,4,192]{3,1,0,2:T(8,128)(2,1)}), bf16[3,145,4,192]{3,1,0,2:T(8,128)(2,1)}, u32[]{:S(2)}, u32[]{:S(2)}) async-start(bf16[3,145,4,192]{3,1,0,2:T(8,128)(2,1)} %copy.169), calls=%async_computation.2 | async-start | bytes 1867776 | tf_op jit(solution)/shard_map/all_to_all | solution.py:329
  930.4 16.0 slice-start
  933.7 12.8 slice-start.1
  933.7 12.8 slice-start.2
  933.7 12.8 slice-start.3
  946.5 6.7 copy-start.4
  961.3 5.1 copy-start.18
  984.1 7.4 copy-start.11
  984.1 46.4 %all-to-all-start.3 = ((bf16[3,580,3,1,192]{4,2,0,3,1:T(4,128)(2,1)}), bf16[3,580,3,1,192]{4,2,0,3,1:T(4,128)(2,1)}, u32[]{:S(2)}, u32[]{:S(2)}) async-start(bf16[3,580,3,1,192]{4,2,0,3,1:T(4,128)(2,1)} %pad_maximum_fusion), calls=%async_computation.3 | async-start | bytes 7127040 | tf_op jit(solution)/shard_map/all_to_all | solution.py:338
  989.8 184.2 %all-reduce.25.cloned.1.call-start = ((), (), s32[]{:S(2)}) async-start(), calls=%async_computation.18 | async-start | bytes 204800
  1036.0 5.7 copy-start.7
  1036.0 5.7 copy-start.39
  1036.0 5.7 copy-start.46
  1041.7 5.2 copy-start.42
  1041.7 6.3 copy-start.48
  1049.3 228.7 %reduce-scatter.11.cloned.1.call-start = ((), (), s32[]{:S(2)}) async-start(), calls=%async_computation.15 | async-start | bytes 2433024 | tf_op jit(solution)/shard_map/reduce_scatter | solution.py:374
  1052.7 350.6 %reduce-scatter.9.cloned.1.call-start = ((), (), s32[]{:S(2)}) async-start(), calls=%async_computation.14 | async-start | bytes 7299072 | tf_op jit(solution)/shard_map/reduce_scatter | solution.py:372
  1060.2 510.7 %reduce-scatter.15.cloned.1.call-start = ((), (), s32[]{:S(2)}) async-start(), calls=%async_computation.17 | async-start | bytes 10616832 | tf_op jit(solution)/shard_map/reduce_scatter | solution.py:386
  1060.9 676.5 %reduce-scatter.13.cloned.1.call-start = ((), (), s32[]{:S(2)}) async-start(), calls=%async_computation.16 | async-start | bytes 10616832 | tf_op jit(solution)/shard_map/reduce_scatter | solution.py:385
  1061.5 3.2 copy-start.15
  1061.5 3.2 copy-start.17
  (30 other events, 45.9 us)
Sparse Core Ops, SparseCore 0:
  10.9 60.4 all-gather.8
  74.3 54.4 all-gather.10
  131.0 35.7 all-gather.14
  179.5 31.4 all-gather.12
  213.0 78.4 all-gather.16
  293.5 78.1 all-gather.18
  788.6 109.2 all-reduce.26
  1049.4 124.6 all-reduce.24
  1179.9 98.0 reduce-scatter.10
  1285.0 118.2 reduce-scatter.8
  1407.4 163.3 reduce-scatter.14
  1574.8 162.5 reduce-scatter.12
where the time goes:
time: 1760 us; the launch traced here: 1740 us
  waiting for transfers between devices  875 us (50%)
  local copies, waits for them, and re-layouts  300 us (17%)
  matrix products  265 us (15%)
  blocking collectives  127 us (7%)
  other arithmetic  121 us (7%)
  starting transfers between devices  20.4 us (1%)
  loops' own time  20.1 us (1%)
    unnamed x14, waiting for transfers between devices  207 us
    reduce_scatter x1, waiting for transfers between devices, per_device(): lax.psum_scatter(outer_grad, 'fsdp', scatter_dimension=1, tiled=True)  168 us
    reduce_scatter x1, waiting for transfers between devices, per_device(): lax.psum_scatter(inner_grad, 'fsdp', scatter_dimension=1, tiled=True)  167 us
    reduce_scatter x1, waiting for transfers between devices, per_device(): lax.psum_scatter(qkv_weight_grad, ('fsdp', 'seq'), scatter_dimension=0, t...  125 us
    reduce_scatter x1, waiting for transfers between devices, per_device(): lax.psum_scatter(proj_weight_grad, ('fsdp', 'seq'), scatter_dimension=0,...  92.4 us
    dot_general x10, matrix products, expert_pass(): jnp.einsum('td,tq->dq', grad_now, active_now, preferred_element_type=jnp....  49.2 us
    unnamed x2, blocking collectives  48.6 us
    dot_general x10, matrix products, expert_pass(): jnp.einsum('td,tq->dq', rows_now, grad_pre, preferred_element_type=jnp.fl...  48.5 us
  transfers between devices with their start and end apart: 16, of which 11 were waited for; matrix products, arithmetic and copies ran while one was open for 14% of the time, Pallas kernels for 0%

commit v1 on v0

--- a/solution.py
+++ b/solution.py
@@ -2,15 +2,960 @@
 
 import jax
 import jax.numpy as jnp
+import numpy as np
 from jax import lax
+from jax.experimental import pallas as pl
+from jax.experimental.pallas import tpu as pltpu
 from jax.sharding import PartitionSpec as P
 
 HEAD = 64
-TILE = 512
-
-
 EPSILON = 1e-06
 HIGHEST = lax.Precision.HIGHEST
+BF, F32 = jnp.bfloat16, jnp.float32
+MESH = pl.DeviceIdType.MESH
+GELU_K = float(np.sqrt(2.0 / np.pi))
+GELU_C = 0.044715
+VMEM = pl.BlockSpec(memory_space=pltpu.VMEM)
+ANY = pl.BlockSpec(memory_space=pl.ANY)
+LIMIT = 60 * 2**20
+
+
+def dot(a, b):
+    return lax.dot_general(a, b, (((1,), (0,)), ((), ())), preferred_element_type=F32)
+
+
+def dot_t(a, b):
+    return lax.dot_general(a, b, (((1,), (1,)), ((), ())), preferred_element_type=F32)
+
+
+def span(start, size):
+    return pl.ds(pl.multiple_of(start, 16), size)
+
+
+class Net:
+    def __init__(self, fsdp):
+        self.f, self.s = lax.axis_index("fsdp"), lax.axis_index("seq")
+        f, s = self.f, self.s
+        self.zn = fsdp // 2
+        self.z, self.x = f // 2, f % 2
+        self.s1 = (s // 2) * 2 + 1 - s % 2
+        self.s2 = (1 - s // 2) * 2 + s % 2
+        self.s3 = 3 - s
+        self.core, self.yp, self.dg = (f, self.s1), (f, self.s2), (f, self.s3)
+        self.xp = (self.z * 2 + 1 - self.x, s)
+        self.zk = [(self.z + k) % self.zn for k in range(1, self.zn)]
+        self.zp = [(zz * 2 + self.x, s) for zz in self.zk]
+        self.zsrc = [(self.z + self.zn - k) % self.zn for k in range(1, self.zn)]
+        self.seqs = [(self.s1, self.core), (self.s2, self.yp), (self.s3, self.dg)]
+
+    def greet(self):
+        barrier = pltpu.get_barrier_semaphore()
+        partners = [self.core, self.yp, self.dg, self.xp] + self.zp
+        for device in partners:
+            pl.semaphore_signal(barrier, inc=1, device_id=device, device_id_type=MESH)
+        pl.semaphore_wait(barrier, len(partners))
+
+
+def rcopy(src, dst, sems, index, device):
+    send, recv = sems
+    copy = pltpu.make_async_remote_copy(
+        src_ref=src,
+        dst_ref=dst,
+        send_sem=send.at[index],
+        recv_sem=recv.at[index],
+        device_id=device,
+        device_id_type=MESH,
+    )
+    copy.start()
+    return copy
+
+
+def lcopy(src, dst, sem):
+    copy = pltpu.make_async_copy(src, dst, sem)
+    copy.start()
+    return copy
+
+
+def norm_parts(values):
+    centred = values - jnp.mean(values, axis=-1, keepdims=True)
+    scale = lax.rsqrt(jnp.mean(centred * centred, axis=-1, keepdims=True) + EPSILON)
+    return centred * scale, scale
+
+
+def lanes(rows):
+    return lax.broadcasted_iota(jnp.int32, (rows, 128), 1)
+
+
+def half_masks():
+    lane = lanes(1)
+    low = jnp.where(lane < HEAD, 1.0, 0.0).astype(BF)
+    return low, jnp.where(lane < HEAD, 0.0, 1.0).astype(BF)
+
+
+def soft_columns(scores):
+    weights = jnp.exp(scores - jnp.max(scores, axis=0, keepdims=True))
+    return weights * (1.0 / jnp.sum(weights, axis=0, keepdims=True))
+
+
+def forward_kernel(
+    dims,
+    x_own, wq_own, wp_own, mask, key_bias, pick, place, c_own, win_own, wout_own,
+    h1, qkv, att, h2, mid, gate, router, w6, wp, sm, c_img, w_in, w_out,
+    x_img, qs, wps, w32, p32, sm32, wr, vt, *sems,
+):
+    fsdp, images, sp, experts, shard = dims
+    net = Net(fsdp)
+    f, s, z, x = net.f, net.s, net.z, net.x
+    img = 4 * sp
+    rowblock = w_in.shape[1] // fsdp
+    (a2a, tok, cot, qg, qf, pg, pf, ps, wg, wf, at) = zip(sems[0:22:2], sems[1:22:2])
+    local = sems[22]
+    open_copies = []
+
+    def go(*args):
+        copy = rcopy(*args)
+        open_copies.append(copy)
+        return copy
+
+    def own_rows(i, who):
+        return span(img * i + sp * who, sp)
+
+    net.greet()
+    first = [go(wq_own.at[who], qs.at[f, s], a2a, k, dev) for k, (who, dev) in enumerate(net.seqs)]
+    keep = [lcopy(wq_own.at[s], qs.at[f, s], local.at[0]), lcopy(wp_own, wps.at[s, f], local.at[1])]
+    toks, cots = [], []
+    for i in range(images):
+        keep.append(lcopy(x_own.at[i], x_img.at[own_rows(i, s)], local.at[2 + i]))
+        toks.append([go(x_own.at[i], x_img.at[own_rows(i, s)], tok, k * images + i, dev) for k, dev in enumerate((net.core, net.yp))])
+    for c in first:
+        c.wait_recv()
+    keep[0].wait()
+    q_z = [go(qs.at[f], qs.at[f], qg, k + 1, dev) for k, dev in enumerate(net.zp)]
+    q_x = [go(qs.at[f], qs.at[f], qg, 0, net.xp)]
+    keep[1].wait()
+    p_z = [go(wps.at[s, f], wps.at[s, f], pg, k + 1, dev) for k, dev in enumerate(net.zp)]
+    p_x = [go(wps.at[s, f], wps.at[s, f], pg, 0, net.xp)]
+    pieces = 2 * experts
+    own = [(win_own, wout_own)[p % 2].at[p // 2] for p in range(pieces)]
+    whole = [(w_in, w_out)[p % 2].at[p // 2] for p in range(pieces)]
+
+    def rows_of(p, who):
+        return whole[p].at[span(rowblock * who, rowblock)]
+
+    w_z, w_x = [None] * pieces, [None] * pieces
+
+    def send_z(p):
+        w_z[p] = [go(own[p], rows_of(p, f), wg, p * fsdp + k + 1, dev) for k, dev in enumerate(net.zp)]
+
+    def send_x(p):
+        w_x[p] = [go(own[p], rows_of(p, f), wg, p * fsdp, net.xp)]
+        keep.append(lcopy(own[p], rows_of(p, f), local.at[2 + 2 * images + p]))
+
+    def pump(p):
+        for k, zz in enumerate(net.zsrc):
+            w_z[p][k].wait_recv()
+            block = rows_of(p, zz * 2 + x)
+            w_x[p].append(go(block, block, wf, p * fsdp + k, net.xp))
+
+    send_z(0)
+    send_z(1)
+    for i in range(images):
+        toks[i][1].wait_recv()
+        rows = own_rows(i, net.s2)
+        toks[i].append(go(x_img.at[rows], x_img.at[rows], tok, 2 * images + i, net.core))
+    for k, zz in enumerate(net.zsrc):
+        q_z[k].wait_recv()
+        q_x.append(go(qs.at[zz * 2 + x], qs.at[zz * 2 + x], qf, k, net.xp))
+    for k, zz in enumerate(net.zsrc):
+        p_z[k].wait_recv()
+        block = wps.at[s, zz * 2 + x]
+        p_x.append(go(block, block, pf, k, net.xp))
+    for p in range(pieces):
+        send_x(p)
+        if p > 1:
+            send_z(p)
+    for i in range(images):
+        cots.append([go(c_own.at[i], c_img.at[own_rows(i, s)], cot, k * images + i, dev) for k, dev in enumerate((net.core, net.yp))])
+        keep.append(lcopy(c_own.at[i], c_img.at[own_rows(i, s)], local.at[2 + images + i]))
+    for c in q_x:
+        c.wait_recv()
+
+    low, high = half_masks()
+    qk_width = w32.shape[1]
+
+    def unpack(d, carry):
+        block = qs[d // 4, d % 4].astype(F32)
+        w32[pl.ds(pl.multiple_of(shard * d, 8), shard), :] = block[:shard]
+        sm32[d] = block[shard:]
+        return carry
+
+    lax.fori_loop(0, 4 * fsdp, unpack, 0)
+    w6[:, 0:384] = w32[:, 0:384].astype(BF)
+    third = w32[:, 384:512]
+    w6[:, 384:512] = third.astype(BF) * low
+    w6[:, 512:640] = pltpu.roll(third, HEAD, 1).astype(BF) * low
+    w6[:, 640:768] = w32[:, 512:640].astype(BF)
+    width = w6.shape[0]
+    devices = 4 * fsdp
+    device = lax.broadcasted_iota(jnp.int32, (devices, width), 0)
+
+    def expand(row, lane, picker, places):
+        spread = dot(sm32[:, row, lane : lane + 128].astype(BF), pick[picker])
+        return jnp.where(device == places, spread, 0.0)
+
+    for r in range(5):
+        sm[r : r + 1, :] = jnp.sum(expand(0, 128 * r, 0, place[0:1, :]), axis=0, keepdims=True)
+    sm[5:6, :] = jnp.sum(expand(1, 0, 1, place[1:2, :] + 4 * s), axis=0, keepdims=True)
+    spread_out = dot(sm32[:, 1, 128:256].astype(BF), pick[2])
+    per_expert = devices // experts
+    wr[...] = jnp.zeros(wr.shape, BF)
+    for e in range(experts):
+        sm[8 + e : 9 + e, :] = jnp.sum(
+            jnp.where(device == place[2:3, :] + per_expert * e, spread_out, 0.0), axis=0, keepdims=True
+        )
+        half = width // 2
+        for j in range(2):
+            sm[12 + e : 13 + e, half * j : half * (j + 1)] = sm32[per_expert * e + 2 * s + j, 1:2, 256 : 256 + half]
+        sm[16 + e : 17 + e, :] = jnp.sum(expand(2, 128 * e, 0, place[0:1, :]), axis=0, keepdims=True)
+    wr[0:8, :] = jnp.concatenate([sm[16:20, :], jnp.zeros((4, width), F32)], axis=0).astype(BF)
+
+    scale_row = jnp.where(lax.broadcasted_iota(jnp.int32, (1, width), 1) % 384 < 128, HEAD**-0.5, 1.0)
+    gain_one, shift_one = sm[0:1, :], sm[1:2, :]
+
+    for c in keep[2 : 2 + images]:
+        c.wait()
+    for i in range(images):
+        toks[i][0].wait_recv()
+        toks[i][2].wait_recv()
+
+        def first_norm(j, carry):
+            rows = span(img * i + sp * j, sp)
+            normed, _ = norm_parts(x_img[rows, :].astype(F32))
+            h1[rows, :] = (normed * gain_one + shift_one).astype(BF)
+            return carry
+
+        lax.fori_loop(0, 4, first_norm, 0)
+        here = pl.ds(img * i, img)
+        for n in range(3):
+            cols = slice(256 * n, 256 * n + 256)
+            part = dot(h1[here, :], w6[:, cols]) + sm[5:6, cols]
+            qkv[here, cols] = (part * scale_row[:, cols]).astype(BF)
+    pump(0)
+
+    def attend(i):
+        base = img * i
+        here = pl.ds(base, img)
+        vt[0] = qkv[here, 256:384].astype(F32).T.astype(BF)
+        vt[1] = qkv[here, 640:768].astype(F32).T.astype(BF)
+
+        def chunk(c, carry):
+            rows = span(base + 128 * c, 128)
+            q01, q2 = qkv[rows, 0:128], qkv[rows, 384:512]
+            outs = []
+            for q, cols, t in ((q01 * low, 128, 0), (q01 * high, 128, 0), (q2, 512, 1)):
+                scores = dot_t(qkv[here, cols : cols + 128], q) + key_bias[...]
+                outs.append(dot(vt[t], soft_columns(scores).astype(BF)))
+            both = jnp.concatenate([outs[0][:HEAD], outs[1][HEAD:]], axis=0)
+            att[s, rows, 0:128] = both.T.astype(BF)
+            att[s, rows, 128:256] = outs[2].T.astype(BF)
+            return carry
+
+        lax.fori_loop(0, img // 128, chunk, 0)
+
+    att_sent = []
+    for i in range(images):
+        attend(i)
+        rows = pl.ds(img * i, img)
+        att_sent.append([go(att.at[s, rows], att.at[s, rows], at, k * images + i, dev) for k, dev in enumerate((net.core, net.yp))])
+        if i > 0:
+            att_sent[i - 1][1].wait_recv()
+            rows = pl.ds(img * (i - 1), img)
+            att_sent[i - 1].append(go(att.at[net.s2, rows], att.at[net.s2, rows], at, 2 * images + i - 1, net.core))
+        pump(i + 1)
+    p_rows = pl.ds(0, fsdp)
+    for c in p_x:
+        c.wait_recv()
+    block = wps.at[s, p_rows]
+    p_seq = [go(wps.at[s], wps.at[s], ps, k, dev) for k, dev in enumerate((net.core, net.yp))]
+    p_seq[1].wait_recv()
+    p_seq.append(go(wps.at[net.s2], wps.at[net.s2], ps, 2, net.core))
+    att_sent[-1][1].wait_recv()
+    rows = pl.ds(img * (images - 1), img)
+    att_sent[-1].append(go(att.at[net.s2, rows], att.at[net.s2, rows], at, 3 * images - 1, net.core))
+    p_seq[0].wait_recv()
+    p_seq[2].wait_recv()
+
+    def unpack_proj(d, carry):
+        p32[pl.ds(pl.multiple_of(shard * d, 8), shard), :] = wps[d % 4, d // 4].astype(F32)[:shard]
+        return carry
+
+    lax.fori_loop(0, 4 * fsdp, unpack_proj, 0)
+    wp[...] = p32[...].astype(BF)
+
+    gain_two, shift_two, proj_shift = sm[2:3, :], sm[3:4, :], sm[4:5, :]
+    group = width // 4
+    tile = img // 2
+    for i in range(images):
+        att_sent[i][0].wait_recv()
+        att_sent[i][2].wait_recv()
+
+        def after(j, carry):
+            rows = span(img * i + tile * j, tile)
+            total = x_img[rows, :].astype(F32) + proj_shift
+            for g in range(4):
+                total += dot(att[g, rows, 0:group], wp[group * g : group * (g + 1), :])
+            mid[rows, :] = total
+            normed, _ = norm_parts(total)
+            low_rows = (normed * gain_two + shift_two).astype(BF)
+            h2[rows, :] = low_rows
+            lane = lanes(tile)
+            logits = jnp.where(lane < experts, dot_t(low_rows, wr[...]), -1e30)
+            weights = jnp.exp(logits - jnp.max(logits, axis=1, keepdims=True))
+            probs = weights * (1.0 / jnp.sum(weights, axis=1, keepdims=True))
+            router[rows, :] = probs
+            gate[rows, :] = probs.astype(BF).astype(F32) * mask[rows, :]
+            return carry
+
+        lax.fori_loop(0, 2, after, 0)
+        if images + 1 + i < pieces:
+            pump(images + 1 + i)
+    for i in range(images):
+        cots[i][1].wait_recv()
+        rows = own_rows(i, net.s2)
+        cots[i].append(go(c_img.at[rows], c_img.at[rows], cot, 2 * images + i, net.core))
+    for p in range(2 * images + 1, pieces):
+        pump(p)
+    for i in range(images):
+        cots[i][0].wait_recv()
+        cots[i][2].wait_recv()
+    for p in range(pieces):
+        for c in w_x[p]:
+            c.wait_recv()
+    for c in open_copies:
+        c.wait_send()
+    for c in keep[2 + images :]:
+        c.wait()
+
+
+def run_forward(dims, x_own, wq_own, wp_own, mask, key_bias, pick, place, c_own, win_own, wout_own):
+    fsdp, images, sp, experts, shard = dims
+    rows, width = images * 4 * sp, x_own.shape[-1]
+    S = jax.ShapeDtypeStruct
+    counts = [3, 3 * images, 3 * images, fsdp, fsdp, fsdp, fsdp, 3, 2 * experts * fsdp, 2 * experts * fsdp, 3 * images]
+    sems = [pltpu.SemaphoreType.DMA((n,)) for n in counts for _ in range(2)]
+    sems.append(pltpu.SemaphoreType.DMA((2 + 2 * images + 2 * experts,)))
+    return pl.pallas_call(
+        partial(forward_kernel, dims),
+        out_shape=(
+            S((rows, width), BF), S((rows, width), BF), S((4, rows, 256), BF), S((rows, width), BF),
+            S((rows, width), F32), S((rows, 128), F32), S((rows, 128), F32),
+            S((width, width), BF), S((width, width), BF), S((24, width), F32),
+            S((rows, width), BF), S((experts, width, win_own.shape[2]), BF), S((experts, width, wout_own.shape[2]), BF),
+        ),
+        in_specs=[VMEM] * 7 + [ANY] * 3,
+        out_specs=[VMEM] * 10 + [ANY] * 3,
+        scratch_shapes=[
+            pltpu.VMEM((rows, width), BF),
+            pltpu.VMEM((fsdp, 4, 32, 640), BF),
+            pltpu.VMEM((4, fsdp, 32, width), BF),
+            pltpu.VMEM((width, 640), F32),
+            pltpu.VMEM((width, width), F32),
+            pltpu.VMEM((4 * fsdp, 8, 640), F32),
+            pltpu.VMEM((128, width), BF),
+            pltpu.VMEM((2, 128, 4 * sp), BF),
+        ] + sems,
+        compiler_params=pltpu.CompilerParams(collective_id=0, has_side_effects=True, vmem_limit_bytes=LIMIT),
+    )(x_own, wq_own, wp_own, mask, key_bias, pick, place, c_own, win_own, wout_own)
+
+
+def pack_rows(values, sp):
+    return jnp.pad(values, ((0, 0), (0, sp - values.shape[1]), (0, 0)))
+
+
+def prepare(t):
+    fsdp, seqs = lax.axis_size("fsdp"), lax.axis_size("seq")
+    s = lax.axis_index("seq")
+    images, slots, width = t["tokens"].shape
+    experts = t["w_in"].shape[0]
+    sp = (slots + 15) // 16 * 16
+    shard = t["w_qkv"].shape[0]
+    dims = (fsdp, images, sp, experts, shard)
+    slot = np.arange(slots)
+    own_valid = ((s == 0) | (slot < slots - 1))[None, :, None]
+    c_own = pack_rows(jnp.where(own_valid, t["cotangent"], jnp.zeros((), BF)), sp)
+    x_own = pack_rows(t["tokens"], sp)
+    split = t["w_qkv"].reshape(shard, 3, seqs, 192)
+    parts = [split[:, n, :, :128] for n in range(3)] + [split[:, n, :, 128:] for n in range(3)]
+    cols = jnp.concatenate(parts + [jnp.zeros((shard, seqs, 64), BF)], axis=-1)
+
+    def lane_row(*items):
+        placed = []
+        for item in items:
+            placed.append(jnp.pad(item, (0, -item.shape[0] % 128)))
+        row = jnp.concatenate(placed)
+        return jnp.pad(row, (0, 640 - row.shape[0]))
+
+    small = jnp.stack(
+        [
+            lane_row(t["ln1_gain"], t["ln1_bias"], t["ln2_gain"], t["ln2_bias"], t["b_proj"]),
+            lane_row(t["b_qv"], t["b_out"], t["b_in"]),
+            lane_row(*[t["w_router"][:, e] for e in range(experts)]),
+        ]
+        + [jnp.zeros((640,), BF)] * 5
+    )
+    wq_own = jnp.concatenate([jnp.swapaxes(cols, 0, 1), jnp.broadcast_to(small, (seqs, 8, 640))], axis=1)
+    wp_own = jnp.pad(t["w_proj"], ((0, 32 - shard), (0, 0)))
+    wout_own = jnp.swapaxes(t["w_out"], 1, 2)
+    routes = t["routes"].reshape(images, seqs, slots, 2)
+    chosen = (routes[..., None] == np.arange(128)).astype(F32).sum(axis=3)
+    alive = (np.arange(seqs)[:, None] == 0) | (slot < slots - 1)
+    chosen = jnp.where(alive[None, :, :, None], chosen, 0.0)
+    mask = jnp.pad(chosen, ((0, 0), (0, 0), (0, sp - slots), (0, 0))).reshape(-1, 128)
+    live = np.zeros((seqs, sp), bool)
+    live[:, : slots - 1] = True
+    live[0, slots - 1] = True
+    key_bias = jnp.broadcast_to(jnp.asarray(np.where(live.reshape(-1, 1), 0.0, -1e30), F32), (seqs * sp, 128))
+    lane = np.arange(width)
+    per = t["b_qv"].shape[0]
+    q_lane = np.where(lane % 384 < 128, lane % 384, 0) + np.where(lane >= 384, 128, 0)
+    v_lane = np.where(lane % 384 >= 256, lane % 384 - 256, 0) + np.where(lane >= 384, 128, 0)
+    is_q, is_v = lane % 384 < 128, lane % 384 >= 256
+    live_lane = (is_q | is_v) & ((lane < 384) | (lane % 128 < 64))
+    at = np.where(is_q, q_lane, v_lane)
+    pick = np.zeros((3, 128, width), np.float32)
+    pick[0, lane % shard, lane] = 1
+    pick[1, (at % per)[live_lane], lane[live_lane]] = 1
+    out_shard = t["b_out"].shape[0]
+    pick[2, lane % out_shard, lane] = 1
+    place = np.zeros((8, width), np.int32)
+    place[0], place[2] = lane // shard, lane // out_shard
+    place[1] = at // per + np.where(is_v, width // per, 0)
+    return dims, (
+        x_own, wq_own, wp_own, mask, key_bias, jnp.asarray(pick, BF), jnp.asarray(place), c_own, t["w_in"], wout_own,
+    ), own_valid
+
+
+def reduce_piece(net, go, p, grads, halves, arrived, xs, zs):
+    return go(grads.at[:, 1 - net.x], halves, xs, p, net.xp)
+
+
+def expert_kernel(
+    dims,
+    h2, c, gate, b_in, w_in, w_out,
+    owned, mixed, bias_grad, halves, quarters,
+    win, wout, h2t, ct, dpre, act, mix, back, dots, ring, htmp, qtmp, cs, cr, ys, yr, *sems,
+):
+    fsdp, images, sp, experts, shard = dims
+    net = Net(fsdp)
+    f, s, z, x = net.f, net.s, net.z, net.x
+    img = 4 * sp
+    rows_all, width = h2.shape
+    ff = win.shape[1]
+    xs, zs, core_sems, y_sems = zip(sems[0:8:2], sems[1:8:2])
+    local = sems[8]
+    open_copies = []
+    pieces = 2 * experts
+    slots = ring.shape[0]
+
+    def go(*args):
+        copy = rcopy(*args)
+        open_copies.append(copy)
+        return copy
+
+    def load(e):
+        return [lcopy(w_in.at[e], win, local.at[0]), lcopy(w_out.at[e], wout, local.at[1])]
+
+    weights = load(0)
+    net.greet()
+    mix[...] = jnp.zeros(mix.shape, F32)
+    back[...] = jnp.zeros(back.shape, F32)
+    dots[...] = jnp.zeros(dots.shape, F32)
+    bias_grad[...] = jnp.zeros(bias_grad.shape, F32)
+
+    def turn(j, carry):
+        rows = pl.ds(pl.multiple_of(128 * j, 128), 128)
+        h2t[:, rows] = h2[rows, :].astype(F32).T.astype(BF)
+        ct[:, rows] = c[rows, :].astype(F32).T.astype(BF)
+        return carry
+
+    lax.fori_loop(0, rows_all // 128, turn, 0)
+
+    sent_x, sent_z = [None] * pieces, [None] * pieces
+
+    def ship(p):
+        sent_x[p] = go(ring.at[p % slots, :, 1 - x], halves.at[p], xs, p, net.xp)
+
+    def relay(p):
+        sent_x[p].wait_recv()
+        pltpu.sync_copy(halves.at[p], htmp)
+        sent_z[p] = []
+        for k, zz in enumerate(net.zk):
+            mine = ring.at[p % slots, zz, x]
+            mine[...] = (mine[...].astype(F32) + htmp[zz].astype(F32)).astype(BF)
+            sent_z[p].append(go(mine, quarters.at[p, k], zs, 3 * p + k, net.zp[k]))
+        owned[p] = ring[p % slots, z, x].astype(F32) + htmp[z].astype(F32)
+
+    def finish(p):
+        for copy in sent_z[p]:
+            copy.wait_recv()
+        pltpu.sync_copy(quarters.at[p], qtmp)
+        owned[p] = owned[p] + qtmp[0].astype(F32) + qtmp[1].astype(F32) + qtmp[2].astype(F32)
+
+    tile = img // 2
+    lane = lanes(tile)
+
+    def expert_rows(e, t):
+        rows = span(tile * t, tile)
+        h_rows, c_rows = h2[rows, :], c[rows, :]
+        gates = jnp.sum(jnp.where(lane == e, gate[rows, :], 0.0), axis=1, keepdims=True)
+        inner = jnp.zeros((tile, 1), F32)
+        for n in range(ff // 256):
+            cols = slice(256 * n, 256 * n + 256)
+            pre = dot(h_rows, win[:, cols]) + b_in[e : e + 1, cols]
+            d_act = dot(c_rows, wout[:, cols])
+            square = pre * pre
+            half = 0.5 + 0.5 * jnp.tanh(pre * (GELU_K + (GELU_K * GELU_C) * square))
+            value = pre * half
+            low_value = value.astype(BF).astype(F32)
+            slope = half + value * (1.0 - half) * (2 * GELU_K + (6 * GELU_K * GELU_C) * square)
+            inner += jnp.sum(low_value * d_act, axis=1, keepdims=True)
+            act[rows, cols] = (low_value * gates).astype(BF)
+            d_pre = slope * (d_act * gates)
+            bias_grad[e : e + 1, cols] += jnp.sum(d_pre, axis=0, keepdims=True)
+            dpre[rows, cols] = d_pre.astype(BF)
+        dots[rows, :] += jnp.where(lane == e, inner, 0.0)
+        for n in range(width // 256):
+            cols = slice(256 * n, 256 * n + 256)
+            mix[rows, cols] += dot_t(act[rows, :], wout[cols, :])
+            back[rows, cols] += dot_t(dpre[rows, :], win[cols, :])
+
+    core_sent, y_sent = [], []
+
+    def pack(i, who):
+        rows = span(img * i + sp * who, sp)
+        return mix[rows, :], back[rows, :], dots[rows, :]
+
+    def core_send(i):
+        for k, who in enumerate((net.s1, net.s3)):
+            at = 0
+            for part in pack(i, who):
+                cs[i, k, :, at : at + part.shape[1]] = part.astype(BF)
+                at += part.shape[1]
+            core_sent.append(go(cs.at[i, k], cr.at[i, k], core_sems, 2 * i + k, net.core))
+
+    def y_send(i):
+        core_sent[2 * i + 1].wait_recv()
+        at = 0
+        for part in pack(i, net.s2):
+            cols = slice(at, at + part.shape[1])
+            ys[i, :, cols] = (part + cr[i, 1, :, cols].astype(F32)).astype(BF)
+            at += part.shape[1]
+        y_sent.append(go(ys.at[i], yr.at[i], y_sems, i, net.yp))
+
+    def collect(i):
+        core_sent[2 * i].wait_recv()
+        y_sent[i].wait_recv()
+        at = 0
+        for part in pack(i, s):
+            cols = slice(at, at + part.shape[1])
+            mixed[i, :, cols] = part + cr[i, 0, :, cols].astype(F32) + yr[i, :, cols].astype(F32)
+            at += part.shape[1]
+
+    def grads(e):
+        for which, (left, right) in enumerate(((h2t, dpre), (ct, act))):
+            p = 2 * e + which
+            if p >= slots:
+                sent_x[p - slots].wait_send()
+                for copy in sent_z[p - slots]:
+                    copy.wait_send()
+            for n in range(ff // 256):
+                cols = slice(256 * n, 256 * n + 256)
+                block = dot(left[...], right[:, cols]).astype(BF)
+                ring[p % slots, :, :, :, cols] = block.reshape(net.zn, 2, width // fsdp, 256)
+            ship(p)
+
+    for e in range(experts):
+        for copy in weights:
+            copy.wait()
+        if e < experts - 1:
+            lax.fori_loop(0, 2 * images, lambda t, carry: (expert_rows(e, t), carry)[1], 0)
+            weights = load(e + 1)
+        else:
+            weights = []
+            for i in range(images):
+                lax.fori_loop(2 * i, 2 * i + 2, lambda t, carry: (expert_rows(e, t), carry)[1], 0)
+                core_send(i)
+                if i > 0:
+                    y_send(i - 1)
+            y_send(images - 1)
+        if e > 1:
+            relay(2 * e - 4)
+            relay(2 * e - 3)
+        grads(e)
+    for i in range(images):
+        collect(i)
+    for p in range(2 * experts - 4, pieces):
+        relay(p)
+        finish(p - (2 * experts - 4))
+    for p in range(4, pieces):
+        finish(p)
+    for copy in open_copies:
+        if copy not in ():
+            pass
+    drained = set()
+    for p in range(pieces - slots):
+        drained.update([id(sent_x[p])] + [id(copy) for copy in sent_z[p]])
+    for copy in open_copies:
+        if id(copy) not in drained:
+            copy.wait_send()
+
+
+def run_experts(dims, h2, c, gate, b_in, w_in, w_out):
+    fsdp, images, sp, experts, shard = dims
+    rows, width = h2.shape
+    ff = w_in.shape[2]
+    block = width // fsdp
+    wide = 2 * width + 128
+    pieces = 2 * experts
+    zn = fsdp // 2
+    S = jax.ShapeDtypeStruct
+    counts = [pieces, 3 * pieces, 2 * images, images]
+    sems = [pltpu.SemaphoreType.DMA((n,)) for n in counts for _ in range(2)]
+    sems.append(pltpu.SemaphoreType.DMA((2,)))
+    V = pltpu.VMEM
+    return pl.pallas_call(
+        partial(expert_kernel, dims),
+        out_shape=(
+            S((pieces, block, ff), F32), S((images, sp, wide), F32), S((8, ff), F32),
+            S((pieces, zn, block, ff), BF), S((pieces, zn - 1, block, ff), BF),
+        ),
+        in_specs=[VMEM] * 4 + [ANY] * 2,
+        out_specs=[VMEM] * 3 + [ANY] * 2,
+        scratch_shapes=[
+            V((width, ff), BF), V((width, ff), BF), V((width, rows), BF), V((width, rows), BF),
+            V((rows, ff), BF), V((rows, ff), BF), V((rows, width), F32), V((rows, width), F32), V((rows, 128), F32),
+            V((4, zn, 2, block, ff), BF), V((zn, block, ff), BF), V((zn - 1, block, ff), BF),
+            V((images, 2, sp, wide), BF), V((images, 2, sp, wide), BF), V((images, sp, wide), BF), V((images, sp, wide), BF),
+        ] + sems,
+        compiler_params=pltpu.CompilerParams(collective_id=1, has_side_effects=True, vmem_limit_bytes=LIMIT),
+    )(h2, c, gate, b_in, w_in, w_out)
+
+
+def backward_kernel(
+    dims,
+    wide, sm, key_bias, bias_grad, w6, wp, h1, qkv, x_own, mid, h2, att, c, gate, router, mask,
+    mixed, g_tokens, g_qkv, g_proj, small,
+    mo, ho, co, ao, gate_o, router_o, mask_o, wr, bo, da, a_img, dmid, db, dl, h1t, dqkv, kt, acc, dh1, cs, cr, ys, yr,
+    total_p, total_q, grad_p, grad_q, half_p, half_q, quarter_p, quarter_q, sum_p, sum_q, seq_p, s_sum, s_core, s_y, s_x, s_z, *sems,
+):
+    fsdp, images, sp, experts, shard = dims
+    net = Net(fsdp)
+    f, s, z, x = net.f, net.s, net.z, net.x
+    img = 4 * sp
+    width = w6.shape[0]
+    group = width // 4
+    a_s, core_s, y_s, x_s, z_s, q_s, small_s = zip(sems[0:14:2], sems[1:14:2])
+    local = sems[14]
+    open_copies = []
+
+    def go(*args):
+        copy = rcopy(*args)
+        open_copies.append(copy)
+        return copy
+
+    def at_rows(i, who):
+        return span(img * i + sp * who, sp)
+
+    own_copies = []
+    for n, (src, dst) in enumerate(((mid, mo), (h2, ho), (c, co), (gate, gate_o), (router, router_o), (mask, mask_o))):
+        for i in range(images):
+            own_copies.append(lcopy(src.at[at_rows(i, s)], dst.at[pl.ds(sp * i, sp)], local.at[n * images + i]))
+    for i in range(images):
+        own_copies.append(lcopy(att.at[:, at_rows(i, s)], ao.at[:, pl.ds(sp * i, sp)], local.at[6 * images + i]))
+    net.greet()
+    used = images * sp
+    for ref in (ho, co, db):
+        ref[used:, :] = jnp.zeros((ref.shape[0] - used, width), BF)
+    for ref in (gate_o, dl):
+        ref[used:, :] = jnp.zeros((ref.shape[0] - used, 128), F32)
+    ao[:, used:, :] = jnp.zeros((4, ao.shape[1] - used, 256), BF)
+    da[...] = jnp.zeros(da.shape, BF)
+    small[...] = jnp.zeros(small.shape, F32)
+    wr[...] = jnp.zeros(wr.shape, BF)
+    bo[...] = jnp.zeros(bo.shape, BF)
+    wr[0:8, :] = jnp.concatenate([sm[16:20, :], jnp.zeros((4, width), F32)], axis=0).astype(BF)
+    bo[0:8, :] = jnp.concatenate([sm[8:12, :], jnp.zeros((4, width), F32)], axis=0).astype(BF)
+    for copy in own_copies:
+        copy.wait()
+
+    gain_two = sm[2:3, :]
+    da_sent = []
+    for i in range(images):
+        rows = pl.ds(sp * i, sp)
+        middle, cc = mo[rows, :], co[rows, :]
+        grad32 = cc.astype(F32)
+        g = gate_o[rows, :]
+        mixed[i] = (middle + wide[i, :, 0:width] + dot(g.astype(BF), bo[...])).astype(BF)
+        d_router = (wide[i, :, 2 * width :] + dot_t(cc, bo[...])) * mask_o[rows, :]
+        probs = router_o[rows, :]
+        d_logits = probs * (d_router - jnp.sum(probs * d_router, axis=1, keepdims=True))
+        dl[rows, :] = d_logits
+        d_h2 = wide[i, :, width : 2 * width] + dot(d_logits.astype(BF), wr[...])
+        normed, scale = norm_parts(middle)
+        inner = d_h2 * gain_two
+        change = inner - jnp.mean(inner, axis=1, keepdims=True) - normed * jnp.mean(inner * normed, axis=1, keepdims=True)
+        d_middle = grad32 + change * scale
+        dmid[rows, :] = d_middle
+        branch = d_middle.astype(BF)
+        db[rows, :] = branch
+        small[2:3, :] += jnp.sum(d_h2 * normed, axis=0, keepdims=True)
+        small[3:4, :] += jnp.sum(d_h2, axis=0, keepdims=True)
+        small[4:5, :] += jnp.sum(branch.astype(F32), axis=0, keepdims=True)
+        for j in range(4):
+            da[j, rows, 0:group] = dot_t(branch, wp[group * j : group * (j + 1), :]).astype(BF)
+        for k, (who, dev) in enumerate(net.seqs):
+            da_sent.append(go(da.at[who, rows], a_img.at[at_rows(i, s)], a_s, 3 * i + k, dev))
+        a_img[at_rows(i, s), :] = da[s, rows, :]
+
+    small[8:16, :] = jnp.concatenate(
+        [dot(gate_o[...].T.astype(BF), co[...])[0:4], dot(dl[...].T.astype(BF), ho[...])[0:4]], axis=0
+    )
+    for e in range(experts):
+        small[pl.ds(16 + 4 * e + s, 1), :] = bias_grad[e : e + 1, :]
+    for j in range(4):
+        turned = ao[j].astype(F32).T.astype(BF)
+        total_p[group * j : group * (j + 1), :] = dot(turned, db[...])[0:group]
+    grad_p[...] = total_p[...].astype(BF).reshape(grad_p.shape)
+    sent_p = go(grad_p.at[:, 1 - x], half_p, x_s, 0, net.xp)
+
+    def turn(j, carry):
+        rows = pl.ds(pl.multiple_of(128 * j, 128), 128)
+        h1t[:, rows] = h1[rows, :].astype(F32).T.astype(BF)
+        return carry
+
+    lax.fori_loop(0, h1.shape[0] // 128, turn, 0)
+    total_q[...] = jnp.zeros(total_q.shape, F32)
+
+    def relay(grad, half, quarter, owned, sent, base):
+        sent.wait_recv()
+        copies = []
+        for k, zz in enumerate(net.zk):
+            grad[zz, x] = (grad[zz, x].astype(F32) + half[zz].astype(F32)).astype(BF)
+            copies.append(go(grad.at[zz, x], quarter.at[k], z_s, base + k, net.zp[k]))
+        owned[...] = grad[z, x].astype(F32) + half[z].astype(F32)
+        return copies
+
+    def finish(quarter, owned, copies):
+        for copy in copies:
+            copy.wait_recv()
+        owned[...] += quarter[0].astype(F32) + quarter[1].astype(F32) + quarter[2].astype(F32)
+
+    low, high = half_masks()
+
+    def attend_back(i):
+        base = img * i
+        here = pl.ds(base, img)
+        kt[0] = qkv[here, 128:256].astype(F32).T.astype(BF)
+        kt[1] = qkv[here, 512:640].astype(F32).T.astype(BF)
+        acc[...] = jnp.zeros(acc.shape, F32)
+
+        def chunk(n, carry):
+            rows = span(base + 128 * n, 128)
+            q01, q2 = qkv[rows, 0:128], qkv[rows, 384:512]
+            a01, a2 = a_img[rows, 0:128], a_img[rows, 128:256]
+            outs = []
+            for q, a, col, t in ((q01 * low, a01 * low, 128, 0), (q01 * high, a01 * high, 128, 0), (q2, a2, 512, 1)):
+                probs = soft_columns(dot_t(qkv[here, col : col + 128], q) + key_bias[...])
+                d_probs = dot_t(qkv[here, col + 128 : col + 256], a)
+                inner = jnp.sum(probs * d_probs, axis=0, keepdims=True)
+                d_scores = (probs * (d_probs - inner)).astype(BF)
+                acc[2 * t] += dot(d_scores, q)
+                acc[2 * t + 1] += dot(probs.astype(BF), a)
+                outs.append(dot(kt[t], d_scores))
+            both = jnp.concatenate([outs[0][:HEAD], outs[1][HEAD:]], axis=0)
+            local_rows = span(128 * n, 128)
+            dqkv[local_rows, 0:128] = (both.T * HEAD**-0.5).astype(BF)
+            dqkv[local_rows, 384:512] = (outs[2].T * HEAD**-0.5).astype(BF)
+            return carry
+
+        lax.fori_loop(0, img // 128, chunk, 0)
+        for n, col in enumerate((128, 256, 512, 640)):
+            dqkv[:, col : col + 128] = acc[n].astype(BF)
+
+    core_sent, y_sent = [], []
+
+    def y_send(i):
+        core_sent[2 * i + 1].wait_recv()
+        ys[i] = (dh1[at_rows(i, net.s2), :] + cr[i, 1].astype(F32)).astype(BF)
+        y_sent.append(go(ys.at[i], yr.at[i], y_s, i, net.yp))
+
+    p_z = None
+    column_sum = jnp.zeros((1, width), F32)
+    for i in range(images):
+        for k in range(3):
+            da_sent[3 * i + k].wait_recv()
+        attend_back(i)
+        here = pl.ds(img * i, img)
+        for n in range(width // 256):
+            cols = slice(256 * n, 256 * n + 256)
+            dh1[here, cols] = dot_t(dqkv[...], w6[cols, :])
+        for k, who in enumerate((net.s1, net.s3)):
+            cs[i, k] = dh1[at_rows(i, who), :].astype(BF)
+            core_sent.append(go(cs.at[i, k], cr.at[i, k], core_s, 2 * i + k, net.core))
+        column_sum = column_sum + jnp.sum(dqkv[...].astype(F32), axis=0, keepdims=True)
+        for n in range(width // 256):
+            cols = slice(256 * n, 256 * n + 256)
+            total_q[:, cols] += dot(h1t[:, here], dqkv[:, cols])
+        if i > 0:
+            y_send(i - 1)
+        if i == 0:
+            p_z = relay(grad_p, half_p, quarter_p, sum_p, sent_p, 0)
+    y_send(images - 1)
+    small[pl.ds(32 + s, 1), :] = column_sum
+    blocks = grad_q.shape[:3]
+    grad_q[:, :, :, 0:384] = total_q[:, 0:384].astype(BF).reshape(blocks + (384,))
+    third = total_q[:, 384:512] + pltpu.roll(total_q[:, 512:640], HEAD, 1)
+    grad_q[:, :, :, 384:512] = third.astype(BF).reshape(blocks + (128,))
+    grad_q[:, :, :, 512:640] = total_q[:, 640:768].astype(BF).reshape(blocks + (128,))
+    sent_q = go(grad_q.at[:, 1 - x], half_q, x_s, 1, net.xp)
+    finish(quarter_p, sum_p, p_z)
+
+    def part_rows(who):
+        return pl.ds(pl.multiple_of(shard * who, 8), shard)
+
+    p_seq = [go(sum_p.at[part_rows(who)], seq_p.at[k], q_s, k, dev) for k, (who, dev) in enumerate(net.seqs)]
+
+    gain_one = sm[0:1, :]
+    for i in range(images):
+        core_sent[2 * i].wait_recv()
+        y_sent[i].wait_recv()
+        d_h1 = dh1[at_rows(i, s), :] + cr[i, 0].astype(F32) + yr[i].astype(F32)
+        normed, scale = norm_parts(x_own[i].astype(F32))
+        inner = d_h1 * gain_one
+        change = inner - jnp.mean(inner, axis=1, keepdims=True) - normed * jnp.mean(inner * normed, axis=1, keepdims=True)
+        g_tokens[i] = dmid[pl.ds(sp * i, sp), :] + change * scale
+        small[0:1, :] += jnp.sum(d_h1 * normed, axis=0, keepdims=True)
+        small[1:2, :] += jnp.sum(d_h1, axis=0, keepdims=True)
+
+    s_sum[0] = small[...]
+    hop = go(s_sum.at[0], s_core, small_s, 0, net.core)
+    hop.wait_recv()
+    s_sum[1] = s_sum[0] + s_core[...]
+    hop = go(s_sum.at[1], s_y, small_s, 1, net.yp)
+    q_z = relay(grad_q, half_q, quarter_q, sum_q, sent_q, 3)
+    hop.wait_recv()
+    s_sum[2] = s_sum[1] + s_y[...]
+    hop = go(s_sum.at[2], s_x, small_s, 2, net.xp)
+    for copy in p_seq:
+        copy.wait_recv()
+    g_proj[...] = sum_p[part_rows(s), :] + seq_p[0] + seq_p[1] + seq_p[2]
+    hop.wait_recv()
+    s_sum[3] = s_sum[2] + s_x[...]
+    hops = [go(s_sum.at[3], s_z.at[k], small_s, 3 + k, dev) for k, dev in enumerate(net.zp)]
+    finish(quarter_q, sum_q, q_z)
+    q_seq = [go(sum_q.at[part_rows(who)], g_qkv.at[s], q_s, 3 + k, dev) for k, (who, dev) in enumerate(net.seqs)]
+    g_qkv[s] = sum_q[part_rows(s), :]
+    for copy in hops:
+        copy.wait_recv()
+    small[...] = s_sum[3] + s_z[0] + s_z[1] + s_z[2]
+    for copy in q_seq:
+        copy.wait_recv()
+    for copy in open_copies:
+        copy.wait_send()
+
+
+def run_backward(dims, *operands):
+    fsdp, images, sp, experts, shard = dims
+    rows, width = images * 4 * sp, operands[4].shape[0]
+    zn, block = fsdp // 2, width // fsdp
+    own = (images * sp + 127) // 128 * 128
+    S, V = jax.ShapeDtypeStruct, pltpu.VMEM
+    counts = [3 * images, 2 * images, images, 2, 6, 6, 6]
+    sems = [pltpu.SemaphoreType.DMA((n,)) for n in counts for _ in range(2)]
+    sems.append(pltpu.SemaphoreType.DMA((7 * images,)))
+    return pl.pallas_call(
+        partial(backward_kernel, dims),
+        out_shape=(
+            S((images, sp, width), BF), S((images, sp, width), F32), S((4, shard, 640), F32), S((shard, width), F32), S((40, width), F32),
+        ),
+        in_specs=[VMEM] * 9 + [ANY] * 7,
+        out_specs=[VMEM] * 5,
+        scratch_shapes=[
+            V((own, width), F32), V((own, width), BF), V((own, width), BF), V((4, own, 256), BF),
+            V((own, 128), F32), V((own, 128), F32), V((own, 128), F32), V((128, width), BF), V((128, width), BF),
+            V((4, own, 256), BF), V((rows, 256), BF), V((own, width), F32), V((own, width), BF), V((own, 128), F32),
+            V((width, rows), BF), V((4 * sp, width), BF), V((2, 128, 4 * sp), BF), V((4, 4 * sp, 128), F32), V((rows, width), F32),
+            V((images, 2, sp, width), BF), V((images, 2, sp, width), BF), V((images, sp, width), BF), V((images, sp, width), BF),
+            V((width, width), F32), V((width, width), F32),
+            V((zn, 2, block, width), BF), V((zn, 2, block, 640), BF), V((zn, block, width), BF), V((zn, block, 640), BF),
+            V((zn - 1, block, width), BF), V((zn - 1, block, 640), BF), V((block, width), F32), V((block, 640), F32),
+            V((3, shard, width), F32), V((4, 40, width), F32), V((40, width), F32), V((40, width), F32), V((40, width), F32), V((3, 40, width), F32),
+        ] + sems,
+        compiler_params=pltpu.CompilerParams(collective_id=2, has_side_effects=True, vmem_limit_bytes=LIMIT),
+    )(*operands)
+
+
+def unpack_small(small, t, fsdp, seqs):
+    experts, width = t["w_in"].shape[0], t["tokens"].shape[2]
+    d = lax.axis_index("fsdp") * seqs + lax.axis_index("seq")
+
+    def piece(flat, size):
+        return lax.dynamic_slice_in_dim(flat, d * size, size, 0)
+
+    shard = t["ln1_gain"].shape[0]
+    rows = lax.dynamic_slice(small[0:5], (0, d * shard), (5, shard))
+    router = lax.dynamic_slice(small[12:16], (0, d * shard), (4, shard)).T
+    out_bias = piece(small[8:12].reshape(-1), t["b_out"].shape[0])
+    in_bias = piece(small[16:32].reshape(-1), t["b_in"].shape[0])
+    tiles = small[32:36]
+    q = jnp.concatenate([tiles[:, 0:128], tiles[:, 384:448]], axis=1).reshape(-1)
+    v = jnp.concatenate([tiles[:, 256:384], tiles[:, 640:704]], axis=1).reshape(-1)
+    qv = piece(jnp.concatenate([q, v]), t["b_qv"].shape[0])
+    return rows, router, out_bias, in_bias, qv
+
+
+NAMES = (
+    "tokens", "routes", "ln1_gain", "ln1_bias", "w_qkv", "b_qv", "w_proj", "b_proj", "ln2_gain", "ln2_bias", "w_router",
+    "w_in", "b_in", "w_out", "b_out", "cotangent",
+)
+
+
+def per_device(*args):
+    t = dict(zip(NAMES, args))
+    fsdp, seqs = lax.axis_size("fsdp"), lax.axis_size("seq")
+    dims, operands, own_valid = prepare(t)
+    _, images, sp, experts, shard = dims
+    slots, width = t["tokens"].shape[1:]
+    x_own, mask, key_bias = operands[0], operands[3], operands[4]
+    h1, qkv, att, h2, mid, gate, router, w6, wp, sm, c_img, w_in, w_out = run_forward(dims, *operands)
+    owned, wide, bias_grad, _, _ = run_experts(dims, h2, c_img, gate, sm[12:20], w_in, w_out)
+    mixed, g_tokens, g_qkv, g_proj, small = run_backward(
+        dims, wide, sm, key_bias, bias_grad, w6, wp, h1, qkv, x_own, mid, h2, att, c_img, gate, router, mask
+    )
+    rows, router_grad, out_bias, in_bias, qv = unpack_small(small, t, fsdp, seqs)
+    cols = jnp.swapaxes(g_qkv, 0, 1)
+    parts = [
+        jnp.concatenate([cols[:, :, 128 * n : 128 * n + 128], cols[:, :, 384 + 64 * n : 448 + 64 * n]], axis=2).reshape(shard, -1)
+        for n in range(3)
+    ]
+    owned = owned.reshape((experts, 2) + owned.shape[1:])
+    return (
+        jnp.where(own_valid, mixed[:, :slots], jnp.zeros((), BF)),
+        jnp.where(own_valid, g_tokens[:, :slots], 0.0),
+        rows[0],
+        rows[1],
+        jnp.concatenate(parts, axis=1),
+        qv,
+        g_proj,
+        rows[4],
+        rows[2],
+        rows[3],
+        router_grad,
+        owned[:, 0],
+        in_bias,
+        jnp.swapaxes(owned[:, 1], 1, 2),
+        out_bias,
+    )
 
 
 def norm_rows(values, gain_vector, shift_vector):
@@ -96,7 +1041,7 @@
     return (result, grad_rows_now, inner_grad, outer_grad, bias_grad)
 
 
-def per_device(
+def per_device_general(
     tokens,
     routes,
     ln1_gain,
@@ -205,76 +1150,30 @@
         lax.all_gather(grad_out, "seq", axis=1, tiled=True),
     )
     token_count = images * length
-    entry_expert = routes.reshape(-1)
-    entry_total = entry_expert.shape[0]
-    tile_count = (entry_total + experts * (TILE - 1)) // TILE
-    order = jnp.argsort(entry_expert, stable=True)
-    inverse = jnp.argsort(order)
-    entry_onehot = entry_expert[:, None] == expert_ids
-    counts = jnp.sum(entry_onehot.astype(jnp.int32), axis=0)
-    padded = (counts + TILE - 1) // TILE * TILE
-    padded_end = jnp.cumsum(padded)
-    padded_start = padded_end - padded
-    count_end = jnp.cumsum(counts)
-    count_start = count_end - counts
-    slot_place = jnp.arange(tile_count * TILE)
-    slot_expert = jnp.sum((padded_end[None, :] <= slot_place[:, None]).astype(jnp.int32), axis=1)
-    slot_onehot = slot_expert[:, None] == expert_ids
-    slot_rank = slot_place - jnp.sum(jnp.where(slot_onehot, padded_start, 0), axis=1)
-    slot_live = (slot_expert < experts) & (
-        slot_rank < jnp.sum(jnp.where(slot_onehot, counts, 0), axis=1)
-    )
-    sorted_index = jnp.clip(
-        jnp.sum(jnp.where(slot_onehot, count_start, 0), axis=1) + slot_rank, 0, entry_total - 1
-    )
-    slot_entry = order[sorted_index]
-    slot_token = slot_entry // 2
-    tile_expert = jnp.minimum(slot_expert.reshape(tile_count, TILE)[:, 0], experts - 1)
-    entry_slot = jnp.sum(jnp.where(entry_onehot, padded_start - count_start, 0), axis=1) + inverse
     rows_flat = group_rows.reshape(token_count, width)
     grad_flat = group_grad.reshape(token_count, width)
-    slot_rows = jnp.where(slot_live[:, None], rows_flat[slot_token], jnp.zeros((), jnp.bfloat16))
-    slot_gate = jnp.where(slot_live, group_gates.reshape(-1)[slot_entry].astype(jnp.float32), 0.0)
-    slot_grad = (slot_gate[:, None] * grad_flat[slot_token].astype(jnp.float32)).astype(
-        jnp.bfloat16
-    )
-
-    def expert_tile(totals, pieces):
-        inner_sum, outer_sum, bias_sum = totals
-        rows_now, grad_now, expert_now = pieces
+    group_chosen = (routes.reshape(token_count, 2)[..., None] == expert_ids).astype(jnp.float32)
+    dense_gates = jnp.sum(
+        group_chosen * group_gates.reshape(token_count, 2).astype(jnp.float32)[..., None], axis=1
+    )
+
+    def expert_step(totals, pieces):
+        inner_now, outer_now, bias_now, gate_now = pieces
+        grad_now = (gate_now[:, None] * grad_flat.astype(jnp.float32)).astype(jnp.bfloat16)
         result, grad_rows_now, inner_part, outer_part, bias_part = expert_pass(
-            rows_now,
-            grad_now,
-            inner_weight[expert_now],
-            outer_weight[expert_now],
-            inner_bias[expert_now],
+            rows_flat, grad_now, inner_now, outer_now, bias_now
         )
-        inner_sum = inner_sum.at[expert_now].add(inner_part)
-        outer_sum = outer_sum.at[expert_now].add(outer_part)
-        bias_sum = bias_sum.at[expert_now].add(bias_part)
-        return ((inner_sum, outer_sum, bias_sum), (result, grad_rows_now))
-
-    initial = (
-        jnp.zeros((experts, width, quarter), jnp.float32),
-        jnp.zeros((experts, width, quarter), jnp.float32),
-        jnp.zeros((experts, quarter), jnp.float32),
-    )
-    (inner_grad, outer_grad, inner_bias_grad), (slot_out, slot_back) = lax.scan(
-        expert_tile,
-        initial,
-        (
-            slot_rows.reshape(tile_count, TILE, width),
-            slot_grad.reshape(tile_count, TILE, width),
-            tile_expert,
-        ),
-    )
-    entry_out = slot_out.reshape(-1, width)[entry_slot].reshape(token_count, 2, width)
-    entry_gate = group_gates.reshape(token_count, 2).astype(jnp.float32)
-    partial_mix = jnp.sum(entry_gate[..., None] * entry_out, axis=1).reshape(images, length, width)
-    partial_rows = jnp.sum(
-        slot_back.reshape(-1, width)[entry_slot].reshape(token_count, 2, width), axis=1
-    )
-    entry_dot = jnp.sum(grad_flat.astype(jnp.float32)[:, None, :] * entry_out, axis=-1)
+        mix_sum, rows_sum = totals
+        dots = jnp.sum(grad_flat.astype(jnp.float32) * result, axis=-1)
+        totals = (mix_sum + gate_now[:, None] * result, rows_sum + grad_rows_now)
+        return totals, (inner_part, outer_part, bias_part, dots)
+
+    blank = jnp.zeros((token_count, width), jnp.float32)
+    (partial_mix, partial_rows), (inner_grad, outer_grad, inner_bias_grad, expert_dots) = lax.scan(
+        expert_step, (blank, blank), (inner_weight, outer_weight, inner_bias, dense_gates.T)
+    )
+    partial_mix = partial_mix.reshape(images, length, width)
+    entry_dot = jnp.einsum("et,tke->tk", expert_dots, group_chosen, precision=HIGHEST)
     expert_mix, row_grad, gate_grad = (
         lax.psum_scatter(
             partial_mix.astype(jnp.bfloat16), "seq", scatter_dimension=1, tiled=True
@@ -441,6 +1340,7 @@
         P(None, "seq", "fsdp"),
         P(("fsdp", "seq")),
     )
+    device_program = per_device if dict(mesh.shape) == {"fsdp": 8, "seq": 4} else per_device_general
     return jax.shard_map(
-        per_device, mesh=mesh, in_specs=in_specs, out_specs=out_specs, check_vma=False
-    )
+        device_program, mesh=mesh, in_specs=in_specs, out_specs=out_specs, check_vma=False
+    )

time: 1760 us -> 497 us (0.28)
  the two profiles are of different devices: /device:TPU:25 before, /device:TPU:0 now
where the time goes in v1:
time: 497 us; the launch traced here: 488 us
  Pallas kernels  456 us (92%)
  local copies, waits for them, and re-layouts  21.3 us (4%)
  other arithmetic  9.12 us (2%)
    pallas_call x1, Pallas kernels, run_experts(): pl.pallas_call(partial(expert_kernel, dims), out_shape=(S((pieces, block,...  192 us
    pallas_call x1, Pallas kernels, run_forward(): pl.pallas_call(partial(forward_kernel, dims), out_shape=(S((rows, width),...  171 us
    pallas_call x1, Pallas kernels, run_backward(): pl.pallas_call(partial(backward_kernel, dims), out_shape=(S((images, sp,...  92.9 us

profile of v1, /device:TPU:0, one launch (start us, length us, event | category | flops | bytes accessed | tf_op | source)
XLA Modules:
  0.0 487.6 jit_solution(3906082374917454665)
XLA Ops:
  0.6 0.0 copy-start.1
  0.7 1.1 reshape.63
  1.9 0.0 copy-start.8
  2.0 0.1 concatenate.36
  2.1 0.8 slice_bitcast_fusion.10
  3.0 0.7 pad.56
  3.6 0.2 dynamic-update-slice
  3.8 0.7 pad.57
  4.5 0.2 dynamic-update-slice.1
  4.6 0.7 pad.58
  5.3 0.2 dynamic-update-slice.2
  5.5 0.7 pad.59
  6.1 0.2 dynamic-update-slice.3
  6.3 0.7 pad.60
  7.0 0.2 dynamic-update-slice.4
  7.2 0.7 fusion.4
  8.0 0.7 pad_maximum_fusion.1.wq_own
  8.6 0.7 broadcast_or_fusion
  9.3 0.0 copy-done.1
  9.3 0.1 broadcast_select_fusion
  9.4 0.0 copy-start.7
  9.4 0.9 pad.70.c_own
  10.4 0.0 copy-done.8
  10.4 0.1 eq.19
  10.5 0.3 copy.58
  10.8 1.6 convert_reduce_fusion
  12.4 0.0 copy-done.7
  12.4 0.3 broadcast_select_fusion.1
  12.7 0.0 copy-start.2
  12.7 0.1 copy.73
  12.8 0.0 copy-start.6
  12.8 0.0 copy-start.9
  12.8 1.0 pad.69.clone
  13.9 0.0 copy-done.2
  13.9 0.9 pad.55.x_own
  14.8 0.6 pad.68.wp_own
  15.4 0.9 broadcast_in_dim.62.key_bias
  16.3 171.0 %shard_map.325 = (bf16[1920,768]{1,0:T(8,128)(2,1)}, bf16[1920,768]{1,0:T(8,128)(2,1)}, bf16[4,1920,256]{2,1,0:T(8,128)(2,1)}, bf16[1920,768]{1,0:T(8,128)(2,1)}...) custom-call(bf16[3,160,768]{2,1,0:T(8,128)(2,1)} %pad.55.x_own, ...), custom_call_target="tpu_custom_call" | custom-call | tf_op jit(solution)/shard_map/pallas_call | solution.py:347
  187.2 1.4 slice.117.b_in
  188.7 191.9 %shard_map.326 = (f32[8,96,768]{2,1,0:T(8,128)}, f32[3,160,1664]{2,1,0:T(8,128)}, f32[8,768]{1,0:T(8,128)}, bf16[8,4,96,768]{3,2,1,0:T(8,128)(2,1)}, bf16[8,3,96,768]{3,2,1,0:T(8,128)(2,1)}) custom-call(bf16[1920,768]{1,0:T(8,128)(2,1)} %get-tuple-element.36.h2, bf16[1920,768]{1,0:T(8,128)(2,1)} %get-tuple-element.37.c, f32[1920,128]{1,0:T(8,128)} %get-tuple-element.38.gate, ...), custom_call_target="tpu_custom_call" | custom-call | tf_op jit(solution)/shard_map/pallas_call | solution.py:626
  380.5 92.9 %shard_map.327 = (bf16[3,160,768]{2,1,0:T(8,128)(2,1)}, f32[3,160,768]{2,1,0:T(8,128)}, f32[4,24,640]{2,1,0:T(8,128)}, f32[24,768]{1,0:T(8,128)}, f32[40,768]{1,0:T(8,128)}) custom-call(f32[3,160,1664]{2,1,0:T(8,128)} %get-tuple-element.42.wide, f32[24,768]{1,0:T(8,128)} %get-tuple-element.39.sm, f32[640,128]{1,0:T(8,128)} %broadcast_in_dim.62.key_bias, ...), custom_call_target="tpu_custom_call" | custom-call | tf_op jit(solution)/shard_map/pallas_call | solution.py:876
  473.5 0.7 fusion.20
  474.2 0.7 fusion.21
  474.9 0.1 reshape.69
  474.9 0.1 reshape.68
  475.0 0.6 fusion.14
  475.6 0.9 fusion.15
  476.5 1.0 fusion.16
  477.5 0.1 reshape.65
  477.7 0.1 reshape.66
  477.8 0.0 copy-start.3
  477.8 0.1 reshape.67
  477.9 0.7 pad_maximum_fusion
  478.7 2.7 slice_select_fusion
  481.4 1.0 slice_select_fusion.1
  482.4 0.0 copy-done.4
  482.4 0.7 dynamic_slice.18
  483.1 0.6 dynamic_slice.19
  483.7 0.1 constant_dynamic-slice_fusion
  483.7 0.5 slice_bitcast_fusion.2
  484.3 0.6 dynamic-slice_bitcast_fusion
  484.9 0.0 copy-done
  484.9 1.6 slice_bitcast_fusion
  486.6 0.6 copy.88
  (37 shorter events, 0.4 us)
Async XLA Ops:
  0.6 8.7 %copy-start.1 = (bf16[3,145,768]{2,1,0:T(8,128)(2,1)S(1)}, bf16[3,145,768]{2,1,0:T(8,128)(2,1)}, u32[]{:S(2)}) copy-start(bf16[3,145,768]{2,1,0:T(8,128)(2,1)} %param.37) | copy-start | bytes 2004484
  1.9 8.4 %copy-start.8 = (s32[3,580,2]{1,2,0:T(2,128)S(1)}, s32[3,580,2]{1,2,0:T(2,128)}, u32[]{:S(2)}) copy-start(s32[3,580,2]{1,2,0:T(2,128)} %param.23) | copy-start | bytes 41764
  9.4 3.0 copy-start.7
  12.7 1.2 copy-start.2
  12.8 2.0 copy-start.6
  12.8 2.6 copy-start.9
  477.8 3.6 copy-start.3
  478.6 3.7 copy-start.4
  478.6 6.3 %copy-start = (f32[8,96,768]{2,1,0:T(8,128)S(1)}, f32[8,96,768]{2,1,0:T(8,128)}, u32[]{:S(2)}) copy-start(f32[8,96,768]{2,1,0:T(8,128)} %get-tuple-element.56) | copy-start | bytes 7077892
  484.9 1.7 copy-start.5
